TPU v7x, 32 devices: a whole 2x2x4 slice. The times are simulated.
32 devices in a mesh: ctx: 8 (over y, x, core), wa: 4 (over z).
Axes of the slice: x: 2, y: 2, z: 4, core: 2. Of those that a mesh axis runs over, the one named last changes fastest.
Arguments:
- tokens: bfloat16 [4, 1024, 1536], P('wa', 'ctx'), may hold values from -6 to 6
- cotangent: bfloat16 [4, 1024, 1536], P('wa', 'ctx'), may hold values from -6 to 6
- adapter_index: int32 [4], P('wa'), may hold values from 0 to 3
- deal: int32 [8], replicated, may hold values from 0 to 7, each once
- frozen_qkv_weight: bfloat16 [1536, 2048], P('wa'), may hold values from -0.15625 to 0.15625
- frozen_qkv_bias: bfloat16 [2048], replicated, may hold values from -3 to 3
- frozen_output_weight: bfloat16 [1536, 1536], P('wa'), may hold values from -0.625 to 0.625
- frozen_gate_up_weight: bfloat16 [2, 1536, 8960], P(None, None, 'wa'), may hold values from -0.15625 to 0.15625
- frozen_down_weight: bfloat16 [8960, 1536], P('wa'), may hold values from -0.0625 to 0.0625
- gain_attn: bfloat16 [1536], replicated, may hold values from 0.099609375 to 1.8984375
- gain_mlp: bfloat16 [1536], replicated, may hold values from 0.099609375 to 1.8984375
- a_qkv: bfloat16 [4, 48, 1536], replicated, may hold values from -0.15625 to 0.15625
- b_q: bfloat16 [4, 16, 1536], replicated, may hold values from -0.75 to 0.75
- b_kv: bfloat16 [4, 2, 16, 256], replicated, may hold values from -0.75 to 0.75
- a_o: bfloat16 [4, 16, 1536], replicated, may hold values from -0.15625 to 0.15625
- output_adapter_lift: bfloat16 [4, 16, 1536], replicated, may hold values from -3 to 3
- a_gu: bfloat16 [4, 32, 1536], replicated, may hold values from -0.15625 to 0.15625
- gate_up_adapter_lift: bfloat16 [4, 2, 16, 8960], replicated, may hold values from -0.75 to 0.75
- a_down: bfloat16 [4, 16, 8960], replicated, may hold values from -0.0625 to 0.0625
- down_adapter_lift: bfloat16 [4, 16, 1536], replicated, may hold values from -0.75 to 0.75
Outputs:
- out: bfloat16 [4, 1024, 1536], P('wa', 'ctx')
- grad_tokens: float32 [4, 1024, 1536], P('wa', 'ctx')
- grad_a_qkv: float32 [4, 48, 1536], replicated
- grad_b_q: float32 [4, 16, 1536], replicated
- grad_b_kv: float32 [4, 2, 16, 256], replicated
- grad_a_o: float32 [4, 16, 1536], replicated
- grad_b_o: float32 [4, 16, 1536], replicated
- grad_a_gu: float32 [4, 32, 1536], replicated
- grad_b_gu: float32 [4, 2, 16, 8960], replicated
- grad_a_down: float32 [4, 16, 8960], replicated
- grad_b_down: float32 [4, 16, 1536], replicated
Inputs may be any that keep to these rules, and one draw needn't show every extreme that they name: `deal`: each context index appears once.
All inputs are finite; a program needn't handle non-finite values.
Results may differ from a plain program's by a relative error of at most 0.024.
Values may be sent and summed in bfloat16 or wider, within the bound.
No kernel may reach another device: no remote copies, remote signals or barrier semaphores. Data moves between devices by JAX's collectives and lax.ppermute only.
A program may use at most 320 MiB of HBM per device.

v0:
```python
import math

import jax
import jax.numpy as jnp
from jax import lax
from jax.sharding import PartitionSpec as P

HD = 128


eps = 1e-06
rope_base = 1000000.0
adapter_scale = 2.0
masked_value = -1e30


def matrix_product(left, right):
    return jnp.dot(left, right, preferred_element_type=jnp.float32)


def product_left(left, right):
    return lax.dot_general(
        left, right, (((0,), (0,)), ((), ())), preferred_element_type=jnp.float32
    )


def product_right(left, right):
    return lax.dot_general(
        left, right, (((1,), (1,)), ((), ())), preferred_element_type=jnp.float32
    )


def normed(input_rows, gain):
    return (
        input_rows
        * lax.rsqrt(jnp.mean(input_rows * input_rows, axis=-1, keepdims=True) + eps)
        * gain
    )


def rope_tables(pos, model_width):
    half = model_width // 2
    freq = rope_base ** (-jnp.arange(half, dtype=jnp.float32) * 2.0 / model_width)
    angle = pos.astype(jnp.float32)[:, None] * freq[None, :]
    cosine = jnp.concatenate([jnp.cos(angle), jnp.cos(angle)], axis=-1)[:, None, :]
    sine = jnp.concatenate([jnp.sin(angle), jnp.sin(angle)], axis=-1)[:, None, :]
    return (cosine, sine)


def rotate(values, cosine, sine):
    half = values.shape[-1] // 2
    rolled = jnp.concatenate([-values[..., half:], values[..., :half]], axis=-1)
    return values * cosine + rolled * sine


def unrotate(grads, cosine, sine):
    half = grads.shape[-1] // 2
    turned = grads * sine
    return grads * cosine + jnp.concatenate([turned[..., half:], -turned[..., :half]], axis=-1)


def row_positions(deal, rows, block):
    owner = rows // (2 * block)
    local = rows % (2 * block)
    table = jnp.arange(deal.shape[0], dtype=jnp.int32)
    pair = jnp.sum(jnp.where(owner[:, None] == table[None, :], deal[None, :], 0), axis=1)
    return jnp.where(
        local < block, pair * block + local, (2 * deal.shape[0] - 1 - pair) * block + local - block
    )


def scores_block(queries, keys, query_pos, key_pos, scale):
    scores = jnp.einsum("tkgd,nkd->tkgn", queries, keys, preferred_element_type=jnp.float32) * scale
    mask = key_pos[None, None, None, :] <= query_pos[:, None, None, None]
    return (scores, mask)


def fold_keys(carry, piece, queries, query_pos, deal, block, scale):
    count = piece.shape[0]
    stride = math.gcd(count, 512)
    kvh = queries.shape[1]
    head = queries.shape[3]
    kvd = kvh * head
    key_pos = row_positions(deal, jnp.arange(count, dtype=jnp.int32), block)

    def fold_visit(state, turn):
        first = turn * stride
        rows_kv = lax.dynamic_slice_in_dim(piece, first, stride, 0)
        keys = rows_kv[:, :kvd].reshape(stride, kvh, head)
        values = rows_kv[:, kvd:].reshape(stride, kvh, head)
        scores, mask = scores_block(
            queries, keys, query_pos, lax.dynamic_slice_in_dim(key_pos, first, stride, 0), scale
        )
        top, total, summed = state
        new_top = jnp.maximum(top, jnp.max(jnp.where(mask, scores, masked_value), axis=-1))
        fade = jnp.exp(top - new_top)
        weights = jnp.where(mask, jnp.exp(scores - new_top[..., None]), 0.0)
        total = total * fade + jnp.sum(weights, axis=-1)
        summed = summed * fade[..., None] + jnp.einsum(
            "tkgn,nkd->tkgd",
            weights.astype(jnp.bfloat16),
            values,
            preferred_element_type=jnp.float32,
        )
        return ((new_top, total, summed), None)

    return lax.scan(fold_visit, carry, jnp.arange(count // stride))[0]


def attend_back(queries, query_pos, kv_all, deal, block, lse, d_out, delta, scale):
    count = kv_all.shape[0]
    stride = math.gcd(count, 512)
    kvh = queries.shape[1]
    head = queries.shape[3]
    kvd = kvh * head
    key_pos = row_positions(deal, jnp.arange(count, dtype=jnp.int32), block)

    def attend_visit(d_query, turn):
        first = turn * stride
        rows_kv = lax.dynamic_slice_in_dim(kv_all, first, stride, 0)
        keys = rows_kv[:, :kvd].reshape(stride, kvh, head)
        values = rows_kv[:, kvd:].reshape(stride, kvh, head)
        scores, mask = scores_block(
            queries, keys, query_pos, lax.dynamic_slice_in_dim(key_pos, first, stride, 0), scale
        )
        probs = jnp.where(mask, jnp.exp(scores - lse[..., None]), 0.0)
        d_values = jnp.einsum(
            "tkgn,tkgd->nkd", probs.astype(jnp.bfloat16), d_out, preferred_element_type=jnp.float32
        )
        d_probs = jnp.einsum("tkgd,nkd->tkgn", d_out, values, preferred_element_type=jnp.float32)
        d_scores = (probs * (d_probs - delta[..., None])).astype(jnp.bfloat16)
        d_query = d_query + jnp.einsum(
            "tkgn,nkd->tkgd", d_scores, keys, preferred_element_type=jnp.float32
        )
        d_keys = (
            jnp.einsum("tkgn,tkgd->nkd", d_scores, queries, preferred_element_type=jnp.float32)
            * scale
        )
        return (
            d_query,
            jnp.concatenate([d_keys.reshape(stride, kvd), d_values.reshape(stride, kvd)], axis=1),
        )

    d_query, pieces = lax.scan(
        attend_visit, jnp.zeros(queries.shape, jnp.float32), jnp.arange(count // stride)
    )
    return (d_query * scale, pieces.reshape(count, 2 * kvd))


def per_device(
    tokens,
    cotangent,
    adapter_index,
    deal,
    frozen_qkv_weight,
    frozen_qkv_bias,
    frozen_output_weight,
    frozen_gate_up_weight,
    frozen_down_weight,
    gain_attn,
    gain_mlp,
    a_qkv,
    b_q,
    b_kv,
    a_o,
    output_adapter_lift,
    a_gu,
    gate_up_adapter_lift,
    a_down,
    down_adapter_lift,
):
    rows = tokens.shape[1]
    block = rows // 2
    model_width = tokens.shape[2]
    adapter_rank = b_q.shape[1]
    kvd = b_kv.shape[3]
    head = HD
    heads = model_width // head
    kvh = kvd // head
    group = heads // kvh
    scale = 1.0 / math.sqrt(head)
    chosen = adapter_index[0]
    slots = (jnp.arange(a_qkv.shape[0], dtype=jnp.int32) == chosen).astype(jnp.float32)

    def picked(table):
        return lax.dynamic_index_in_dim(table, chosen, 0, keepdims=False)

    def spread(grad):
        return slots.reshape((slots.shape[0],) + (1,) * grad.ndim) * grad[None]

    sel_aqkv, sel_bq, sel_bkv = (picked(a_qkv), picked(b_q), picked(b_kv))
    sel_ao, selected_output_lift, sel_agu = (picked(a_o), picked(output_adapter_lift), picked(a_gu))
    selected_gate_up_lift, sel_adown, selected_down_lift = (
        picked(gate_up_adapter_lift),
        picked(a_down),
        picked(down_adapter_lift),
    )
    local_rows = lax.axis_index("ctx") * rows + jnp.arange(rows, dtype=jnp.int32)
    query_pos = row_positions(deal, local_rows, block)
    cosine, sine = rope_tables(query_pos, head)
    gain_one = gain_attn.astype(jnp.float32)
    gain_two = gain_mlp.astype(jnp.float32)
    input_tokens = tokens[0].astype(jnp.float32)
    complete_qkv, complete_output = (
        lax.all_gather(frozen_qkv_weight, "wa", axis=0, tiled=True),
        lax.all_gather(frozen_output_weight, "wa", axis=0, tiled=True),
    )
    first_normed = normed(input_tokens, gain_one).astype(jnp.bfloat16)
    qkv_low_rank = product_right(first_normed, sel_aqkv).astype(jnp.bfloat16)
    adapter_extra = jnp.concatenate(
        [
            matrix_product(qkv_low_rank[:, :adapter_rank], sel_bq),
            matrix_product(qkv_low_rank[:, adapter_rank : 2 * adapter_rank], sel_bkv[0]),
            matrix_product(qkv_low_rank[:, 2 * adapter_rank :], sel_bkv[1]),
        ],
        axis=1,
    )
    linear_values = (
        matrix_product(first_normed, complete_qkv)
        + frozen_qkv_bias.astype(jnp.float32)
        + adapter_scale * adapter_extra
    )
    queries = rotate(linear_values[:, :model_width].reshape(rows, heads, head), cosine, sine)
    queries = queries.astype(jnp.bfloat16).reshape(rows, kvh, group, head)
    keys_rot = rotate(
        linear_values[:, model_width : model_width + kvd].reshape(rows, kvh, head), cosine, sine
    ).reshape(rows, kvd)
    kv_mine = jnp.concatenate([keys_rot, linear_values[:, model_width + kvd :]], axis=1).astype(
        jnp.bfloat16
    )
    start_state = (
        jnp.full((rows, kvh, group), masked_value, jnp.float32),
        jnp.zeros((rows, kvh, group), jnp.float32),
        jnp.zeros((rows, kvh, group, head), jnp.float32),
    )
    top, total, summed = fold_keys(
        start_state,
        lax.all_gather(kv_mine, "ctx", axis=0, tiled=True),
        queries,
        query_pos,
        deal,
        block,
        scale,
    )
    lse = top + jnp.log(total)
    attention_output = (summed / total[..., None]).reshape(rows, model_width)
    attention_adapter_low = attention_output.astype(jnp.bfloat16)
    output_low_rank = product_right(attention_adapter_low, sel_ao).astype(jnp.bfloat16)
    middle_rows = (
        input_tokens
        + matrix_product(attention_adapter_low, complete_output)
        + adapter_scale * matrix_product(output_low_rank, selected_output_lift)
    )
    second_normed = normed(middle_rows, gain_two).astype(jnp.bfloat16)
    gate_up_low_rank = product_right(second_normed, sel_agu).astype(jnp.bfloat16)
    grad_out = cotangent[0].astype(jnp.float32)
    low_rank_gradient = grad_out.astype(jnp.bfloat16)
    down_gradient = (adapter_scale * product_right(low_rank_gradient, selected_down_lift)).astype(
        jnp.bfloat16
    )
    complete_gate_up, complete_down = (
        lax.all_gather(frozen_gate_up_weight, "wa", axis=2, tiled=True),
        lax.all_gather(frozen_down_weight, "wa", axis=0, tiled=True),
    )
    gate_values = matrix_product(
        second_normed, complete_gate_up[0]
    ) + adapter_scale * matrix_product(gate_up_low_rank[:, :adapter_rank], selected_gate_up_lift[0])
    upper_values = matrix_product(
        second_normed, complete_gate_up[1]
    ) + adapter_scale * matrix_product(gate_up_low_rank[:, adapter_rank:], selected_gate_up_lift[1])
    sigma = jax.nn.sigmoid(gate_values)
    swish_value = gate_values * sigma
    hidden_state = (swish_value * upper_values).astype(jnp.bfloat16)
    down_low_rank = product_right(hidden_state, sel_adown).astype(jnp.bfloat16)
    result = (
        middle_rows
        + matrix_product(hidden_state, complete_down)
        + adapter_scale * matrix_product(down_low_rank, selected_down_lift)
    ).astype(jnp.bfloat16)
    back_gu, back_down = (
        lax.all_gather(frozen_gate_up_weight, "wa", axis=2, tiled=True),
        lax.all_gather(frozen_down_weight, "wa", axis=0, tiled=True),
    )
    down_lift_gradient = adapter_scale * product_left(down_low_rank, low_rank_gradient)
    grad_adown = product_left(down_gradient, hidden_state)
    d_hidden = product_right(low_rank_gradient, back_down) + matrix_product(
        down_gradient, sel_adown
    )
    d_gate = (d_hidden * upper_values * (sigma * (1.0 + gate_values * (1.0 - sigma)))).astype(
        jnp.bfloat16
    )
    d_upper = (d_hidden * swish_value).astype(jnp.bfloat16)
    d_small_gu = (
        adapter_scale
        * jnp.concatenate(
            [
                product_right(d_gate, selected_gate_up_lift[0]),
                product_right(d_upper, selected_gate_up_lift[1]),
            ],
            axis=1,
        )
    ).astype(jnp.bfloat16)
    gate_up_lift_gradient = adapter_scale * jnp.stack(
        [
            product_left(gate_up_low_rank[:, :adapter_rank], d_gate),
            product_left(gate_up_low_rank[:, adapter_rank:], d_upper),
        ]
    )
    grad_agu = product_left(d_small_gu, second_normed)
    d_normed_two = (
        product_right(d_gate, back_gu[0])
        + product_right(d_upper, back_gu[1])
        + matrix_product(d_small_gu, sel_agu)
    )
    slot_bgu = spread(gate_up_lift_gradient)
    slot_adown = spread(grad_adown)
    pull_two = jax.vjp(normed, middle_rows, gain_two)[1]
    d_mid = grad_out + pull_two(d_normed_two)[0]
    middle_low_rank = d_mid.astype(jnp.bfloat16)
    small_output_gradient = (
        adapter_scale * product_right(middle_low_rank, selected_output_lift)
    ).astype(jnp.bfloat16)
    output_lift_gradient = adapter_scale * product_left(output_low_rank, middle_low_rank)
    grad_ao = product_left(small_output_gradient, attention_adapter_low)
    back_qkv, back_o = (
        lax.all_gather(frozen_qkv_weight, "wa", axis=0, tiled=True),
        lax.all_gather(frozen_output_weight, "wa", axis=0, tiled=True),
    )
    d_attn = (
        product_right(middle_low_rank, back_o) + matrix_product(small_output_gradient, sel_ao)
    ).astype(jnp.bfloat16)
    d_out = d_attn.reshape(rows, kvh, group, head)
    delta = jnp.sum(
        d_out.astype(jnp.float32) * attention_output.reshape(rows, kvh, group, head), axis=-1
    )
    kv_back = lax.all_gather(kv_mine, "ctx", axis=0, tiled=True)
    d_query, d_kv_all = attend_back(
        queries, query_pos, kv_back, deal, block, lse, d_out, delta, scale
    )
    d_kv = lax.psum_scatter(
        d_kv_all.astype(jnp.bfloat16), "ctx", scatter_dimension=0, tiled=True
    ).astype(jnp.float32)
    d_query_pre = unrotate(d_query.reshape(rows, heads, head), cosine, sine).reshape(
        rows, model_width
    )
    d_key_pre = unrotate(d_kv[:, :kvd].reshape(rows, kvh, head), cosine, sine).reshape(rows, kvd)
    linear_gradient = jnp.concatenate([d_query_pre, d_key_pre, d_kv[:, kvd:]], axis=1).astype(
        jnp.bfloat16
    )
    d_small_one = (
        adapter_scale
        * jnp.concatenate(
            [
                product_right(linear_gradient[:, :model_width], sel_bq),
                product_right(linear_gradient[:, model_width : model_width + kvd], sel_bkv[0]),
                product_right(linear_gradient[:, model_width + kvd :], sel_bkv[1]),
            ],
            axis=1,
        )
    ).astype(jnp.bfloat16)
    query_bias_gradient = adapter_scale * product_left(
        qkv_low_rank[:, :adapter_rank], linear_gradient[:, :model_width]
    )
    key_value_bias_gradient = adapter_scale * jnp.stack(
        [
            product_left(
                qkv_low_rank[:, adapter_rank : 2 * adapter_rank],
                linear_gradient[:, model_width : model_width + kvd],
            ),
            product_left(
                qkv_low_rank[:, 2 * adapter_rank :], linear_gradient[:, model_width + kvd :]
            ),
        ]
    )
    grad_aqkv = product_left(d_small_one, first_normed)
    d_normed_one = product_right(linear_gradient, back_qkv) + matrix_product(d_small_one, sel_aqkv)
    pull_one = jax.vjp(normed, input_tokens, gain_one)[1]
    grad_inputs = d_mid + pull_one(d_normed_one)[0]
    totals = lax.psum(
        (
            spread(grad_aqkv),
            spread(query_bias_gradient),
            spread(key_value_bias_gradient),
            spread(grad_ao),
            spread(output_lift_gradient),
            spread(grad_agu),
            slot_bgu,
            slot_adown,
            spread(down_lift_gradient),
        ),
        ("ctx", "wa"),
    )
    return (
        result[None],
        grad_inputs[None],
        totals[0],
        totals[1],
        totals[2],
        totals[3],
        totals[4],
        totals[5],
        totals[6],
        totals[7],
        totals[8],
    )


def solution(mesh):
    return jax.shard_map(
        per_device,
        mesh=mesh,
        in_specs=(
            P("wa", "ctx", None),
            P("wa", "ctx", None),
            P("wa"),
            P(),
            P("wa", None),
            P(),
            P("wa", None),
            P(None, None, "wa"),
            P("wa", None),
            P(),
            P(),
            P(),
            P(),
            P(),
            P(),
            P(),
            P(),
            P(),
            P(),
            P(),
        ),
        out_specs=(
            P("wa", "ctx", None),
            P("wa", "ctx", None),
            P(),
            P(),
            P(),
            P(),
            P(),
            P(),
            P(),
            P(),
            P(),
        ),
        check_vma=False,
    )
```

profile of v0, /device:TPU:0, one launch (start us, length us, event | category | flops | bytes accessed | tf_op | source)
XLA Modules:
  0.0 2031.6 jit_solution(12020353007266106612)
XLA Ops:
  15.7 1.6 fusion.122
  19.9 107.8 %all-gather.6.cloned.1.call-done = bf16[1536,2048]{1,0:T(8,128)(2,1)} async-done(((bf16[384,2048]{1,0:T(8,128)(2,1)}), bf16[1536,2048]{1,0:T(8,128)(2,1)}) %all-gather.6.cloned.1.call-update) | async-done | bytes 6291472 | tf_op jit(solution)/shard_map/all_gather | solution.py:205
  127.7 3.9 fusion.45
  141.0 1.6 fusion.49
  142.6 2.1 slice.152
  144.7 2.3 copy.81
  150.4 8.6 all-gather.8.cloned.1.call-done
  159.0 2.4 copy.83
  161.9 26.2 %while.28 = (s32[]{:T(128)}, f32[128,2,6]{0,2,1:T(8,128)S(1)}, f32[128,2,6]{0,2,1:T(8,128)}, f32[128,2,6,128]{0,3,2,1:T(8,128)}, s32[2]{0:T(128)}, /*index=5*/s3...) while((s32[]{:T(128)}, f32[128,2,6]{0,2,1:T(8,128)S(1)}, ...), condition=%wide.region_6.7_spmd.clone, body=%wide.region_3.6_spmd.clone.sunk | while | flops 411966976 | bytes 26012580 | solution.py:107
  164.0 1.8 fusion.265
  165.8 3.3 fusion.266
  169.2 2.9 fusion.267
  172.4 2.6 fusion.269
  177.2 1.8 fusion.265
  179.0 3.3 fusion.266
  182.3 2.7 fusion.267
  185.2 2.9 fusion.269
  191.1 58.9 %all-gather.10.cloned.1.call-done = bf16[1536,1536]{1,0:T(8,128)(2,1)} async-done(((bf16[384,1536]{1,0:T(8,128)(2,1)}), bf16[1536,1536]{1,0:T(8,128)(2,1)}) %all-gather.10.cloned.1.call-update) | async-done | bytes 4718608 | tf_op jit(solution)/shard_map/all_gather | solution.py:206
  250.0 3.3 convolution_add_fusion.4
  257.4 455.9 %all-gather.14.cloned.1.call-done = bf16[8960,1536]{1,0:T(8,128)(2,1)} async-done(((bf16[2240,1536]{1,0:T(8,128)(2,1)}), bf16[8960,1536]{1,0:T(8,128)(2,1)}) %all-gather.14.cloned.1.call-update) | async-done | bytes 27525136 | tf_op jit(solution)/shard_map/all_gather | solution.py:263
  713.3 18.4 fusion.77
  731.7 895.2 %all-gather.12.cloned.1.call-done = bf16[2,1536,8960]{1,2,0:T(8,128)(2,1)} async-done(((bf16[2,1536,2240]{1,2,0:T(8,128)(2,1)}), bf16[2,1536,8960]{1,2,0:T(8,128)(2,1)}) %all-gather.12.cloned.1.call-update) | async-done | bytes 55050256 | tf_op jit(solution)/shard_map/all_gather | solution.py:262
  1626.9 15.3 fusion.36
  1642.2 5.2 fusion.37
  1647.4 15.5 fusion.34
  1662.9 3.2 fusion.38
  1666.6 6.7 multiply_convert_fusion
  1673.3 1.6 convolution_bitcast_fusion.2
  1678.4 11.6 fusion.33
  1690.1 11.0 fusion.44
  1705.5 1.7 fusion.173
  1710.5 18.2 while.29
  1714.0 2.1 fusion.282
  1716.7 1.8 fusion.284
  1723.0 2.1 fusion.282
  1725.7 1.8 fusion.284
  1731.2 1.6 convolution_convert_fusion.3
  1734.2 2.5 broadcast_multiply_fusion
  1737.8 2.3 copy.87
  1741.6 2.7 broadcast_multiply_fusion.1
  1744.4 30.2 %reduce-scatter.2.cloned.1.call-done = bf16[128,512]{1,0:T(8,128)(2,1)} async-done(((bf16[1024,512]{1,0:T(8,128)(2,1)}), bf16[128,512]{1,0:T(8,128)(2,1)}) %reduce-scatter.2.cloned.1.call-update) | async-done | bytes 131088 | tf_op jit(solution)/shard_map/reduce_scatter | solution.py:340
  1784.4 11.6 convolution_add_fusion.5
  1796.0 1.8 fusion.48
  1799.0 5.3 fusion.67
  1806.8 204.6 %all-reduce.3.cloned.1.call-done = (f32[4,48,1536]{2,1,0:T(8,128)}, f32[4,16,1536]{2,1,0:T(8,128)}, f32[4,2,16,256]{3,2,1,0:T(8,128)}, f32[4,16,1536]{2,1,0:T(8,...) async-done(((f32[4,48,1536]{2,1,0:T(8,128)}, ...) | async-done | bytes 10551312 | tf_op jit(solution)/shard_map/psum | solution.py:379
  2011.4 2.5 copy.148
  2013.9 1.9 copy.149
  2018.8 2.3 copy.154
  (289 shorter events, 80.1 us)
Async XLA Ops:
  7.2 1635.1 %copy-start = (bf16[4,2,16,8960]{3,2,1,0:T(8,128)(2,1)S(1)}, bf16[4,2,16,8960]{3,2,1,0:T(8,128)(2,1)}, u32[]{:S(2)}) copy-start(bf16[4,2,16,8960]{3,2,1,0:T(8,128)(2,1)} %param.41) | copy-start | bytes 6881284
  7.2 120.5 %copy-start.9 = (bf16[1,128,1536]{2,1,0:T(8,128)(2,1)S(1)}, bf16[1,128,1536]{2,1,0:T(8,128)(2,1)}, u32[]{:S(2)}) copy-start(bf16[1,128,1536]{2,1,0:T(8,128)(2,1)} %param.24) | copy-start | bytes 1179652
  7.2 120.5 %all-gather.6.cloned.1.call-start = ((), (), s32[]{:S(2)}) async-start(), calls=%async_computation.1 | async-start | bytes 7864320 | tf_op jit(solution)/shard_map/all_gather | solution.py:205
  7.9 151.0 %all-gather.8.cloned.1.call-start = ((), (), s32[]{:S(2)}) async-start(), calls=%async_computation.2 | async-start | bytes 1179648 | tf_op jit(solution)/shard_map/all_gather | solution.py:238
  9.3 122.2 %copy-start.43 = (f32[1536]{0:T(1024)}, f32[1536]{0:T(1024)S(1)}, u32[]{:S(2)}) copy-start(f32[1536]{0:T(1024)S(1)} %convert_element_type.128) | copy-start | bytes 18436
  11.6 5.6 copy-start.30
  12.4 135.8 %copy-start.28 = (f32[128,128]{0,1:T(8,128)}, f32[128,128]{0,1:T(8,128)S(1)}, u32[]{:S(2)}) copy-start(f32[128,128]{0,1:T(8,128)S(1)} %pad_maximum_fusion.3) | copy-start | bytes 196612
  14.3 117.3 %copy-start.61 = (f32[128]{0:T(128)}, f32[128]{0:T(128)S(1)}, u32[]{:S(2)}) copy-start(f32[128]{0:T(128)S(1)} %fusion.166) | copy-start | bytes 1540
  137.1 112.9 %all-gather.10.cloned.1.call-start = ((), (), s32[]{:S(2)}) async-start(), calls=%async_computation.3 | async-start | bytes 5898240 | tf_op jit(solution)/shard_map/all_gather | solution.py:206
  137.8 575.5 %all-gather.14.cloned.1.call-start = ((), (), s32[]{:S(2)}) async-start(), calls=%async_computation.5 | async-start | bytes 34406400 | tf_op jit(solution)/shard_map/all_gather | solution.py:263
  138.4 1488.5 %all-gather.12.cloned.1.call-start = ((), (), s32[]{:S(2)}) async-start(), calls=%async_computation.4 | async-start | bytes 68812800 | tf_op jit(solution)/shard_map/all_gather | solution.py:262
  139.0 1635.5 %reduce-scatter.2.cloned.1.call-start = ((), (), s32[]{:S(2)}) async-start(), calls=%async_computation.6 | async-start | bytes 1179648 | tf_op jit(solution)/shard_map/reduce_scatter | solution.py:340
  161.9 3.9 copy-start.45
  161.9 3.9 copy-start.49
  175.0 3.9 copy-start.45
  175.1 3.9 copy-start.49
  191.0 63.5 %copy-start.37 = (f32[128,2,6]{0,2,1:T(8,128)S(1)}, f32[128,2,6]{0,2,1:T(8,128)}, u32[]{:S(2)}) copy-start(f32[128,2,6]{0,2,1:T(8,128)} %get-tuple-element.119) | copy-start | bytes 18436
  191.1 64.3 %copy-start.48 = (f32[1536]{0:T(1024)S(1)}, f32[1536]{0:T(1024)}, u32[]{:S(2)}) copy-start(f32[1536]{0:T(1024)} %convert_element_type.140) | copy-start | bytes 18436
  1662.9 3.7 copy-start.19
  1662.9 3.7 copy-start.58
  1678.4 27.0 %slice-start = ((s8[4718592]{0:T(1024)(128)(4,1)}), s8[4194304]{0:T(1024)(128)(4,1)S(1)}, s32[]{:S(2)}) async-start(s8[4718592]{0:T(1024)(128)(4,1)} %bitcast.358), calls=%async_computation.8 | async-start | bytes 8388608
  1690.0 11.1 copy-start.7
  1690.0 12.4 copy-start.13
  1690.1 15.4 slice-start.1
  1702.7 4.4 copy-start.4
  1710.5 18.4 copy-start.31
  1729.7 4.4 copy-start.17
  1729.8 4.4 copy-start.23
  1729.8 4.4 copy-start.24
  1731.2 49.9 %copy-start.53 = (f32[128,16]{0,1:T(8,128)}, f32[128,16]{0,1:T(8,128)S(1)}, u32[]{:S(2)}) copy-start(f32[128,16]{0,1:T(8,128)S(1)} %fusion.107) | copy-start | bytes 24580
  1740.1 36.0 %copy-start.34 = (f32[128,128]{1,0:T(8,128)S(1)}, f32[128,128]{1,0:T(8,128)}, u32[]{:S(2)}) copy-start(f32[128,128]{1,0:T(8,128)} %copy.80) | copy-start | bytes 196612
  1740.1 271.3 %all-reduce.3.cloned.1.call-start = ((), (), s32[]{:S(2)}) async-start(), calls=%async_computation.7 | async-start | bytes 21102592 | tf_op jit(solution)/shard_map/psum | solution.py:379
  1740.4 36.3 %copy-start.27 = (f32[128,2,128]{2,1,0:T(2,128)S(1)}, f32[128,2,128]{2,1,0:T(2,128)}, u32[]{:S(2)}) copy-start(f32[128,2,128]{2,1,0:T(2,128)} %copy-done.26) | copy-start | bytes 393220
  1741.6 40.1 %copy-start.10 = (bf16[1,128,1536]{2,1,0:T(8,128)(2,1)S(1)}, bf16[1,128,1536]{2,1,0:T(8,128)(2,1)}, u32[]{:S(2)}) copy-start(bf16[1,128,1536]{2,1,0:T(8,128)(2,1)} %param.24) | copy-start | bytes 1179652
  1741.6 40.1 %copy-start.44 = (f32[1536]{0:T(1024)S(1)}, f32[1536]{0:T(1024)}, u32[]{:S(2)}) copy-start(f32[1536]{0:T(1024)} %copy-done.43) | copy-start | bytes 18436
  1741.6 40.1 %copy-start.62 = (f32[128]{0:T(128)S(1)}, f32[128]{0:T(128)}, u32[]{:S(2)}) copy-start(f32[128]{0:T(128)} %copy-done.61) | copy-start | bytes 1540
  1778.4 4.9 copy-start.55
  1798.9 5.4 copy-start.54
  1799.0 5.4 copy-start.56
  1799.0 5.4 copy-start.60
  1799.0 6.7 copy-start.65
  1799.0 6.7 copy-start.5
  2011.4 4.4 copy-start.47
  2011.4 5.1 copy-start.42
  2011.4 5.8 copy-start.41
  2011.4 6.6 copy-start.32
  2011.4 7.4 copy-start.18
  2018.8 5.4 copy-start.1
  (34 other events, 76.9 us)
Sparse Core Ops, SparseCore 0:
  9.6 118.0 all-gather.5
  137.2 21.7 all-gather.7
  160.6 89.3 all-gather.9
  251.4 461.8 all-gather.13
  714.8 912.1 all-gather.11
  1740.2 34.2 reduce-scatter.1
  1783.4 227.8 all-reduce.2
where the time goes:
time: 2040 us; the launch traced here: 2030 us
  waiting for transfers between devices  1760 us (86%)
  matrix products  168 us (8%)
  local copies, waits for them, and re-layouts  44.7 us (2%)
  other arithmetic  36 us (2%)
    all_gather x1, waiting for transfers between devices, per_device(): lax.all_gather(frozen_gate_up_weight, 'wa', axis=2, tiled=True)  895 us
    all_gather x1, waiting for transfers between devices, per_device(): lax.all_gather(frozen_down_weight, 'wa', axis=0, tiled=True)  456 us
    psum x1, waiting for transfers between devices, per_device(): lax.psum((spread(grad_aqkv), spread(query_bias_gradient), spread(key_valu...  205 us
    all_gather x1, waiting for transfers between devices, per_device(): lax.all_gather(frozen_qkv_weight, 'wa', axis=0, tiled=True)  108 us
    dot_general x16, matrix products, matrix_product(): return jnp.dot(left, right, preferred_element_type=jnp.float32)  75.6 us
    dot_general x16, matrix products, product_right(): lax.dot_general(left, right, (((1,), (1,)), ((), ())), preferred_element_...  60 us
    all_gather x1, waiting for transfers between devices, per_device(): lax.all_gather(frozen_output_weight, 'wa', axis=0, tiled=True)  58.9 us
  transfers between devices with their start and end apart: 7, of which 7 were waited for; matrix products, arithmetic and copies ran while one was open for 5% of the time, Pallas kernels for 0%

commit v1 on v0

v1 whole, which is shorter than its diff:
```python
import math

import jax
import jax.numpy as jnp
from jax import lax
from jax.sharding import PartitionSpec as P

HD = 128
EPS = 1e-06
ROPE_BASE = 1000000.0
ADAPTER_SCALE = 2.0
MASKED = -1e30
F32 = jnp.float32
BF16 = jnp.bfloat16


def dot_nn(a, b):
    return lax.dot_general(a, b, (((1,), (0,)), ((), ())), preferred_element_type=F32)


def dot_tn(a, b):
    return lax.dot_general(a, b, (((0,), (0,)), ((), ())), preferred_element_type=F32)


def dot_nt(a, b):
    return lax.dot_general(a, b, (((1,), (1,)), ((), ())), preferred_element_type=F32)


def inverse_norm(rows):
    return lax.rsqrt(jnp.mean(rows * rows, axis=-1, keepdims=True) + EPS)


def norm_pull(rows, inv, gain, grad):
    scaled = gain * grad
    return inv * scaled - rows * (inv * inv * inv) * jnp.mean(rows * scaled, axis=-1, keepdims=True)


def rope_tables(pos):
    half = HD // 2
    freq = ROPE_BASE ** (-jnp.arange(half, dtype=F32) * 2.0 / HD)
    angle = pos.astype(F32)[:, None] * freq[None, :]
    cosine = jnp.concatenate([jnp.cos(angle), jnp.cos(angle)], axis=-1)[:, None, :]
    sine = jnp.concatenate([jnp.sin(angle), jnp.sin(angle)], axis=-1)[:, None, :]
    return cosine, sine


def rotate(values, cosine, sine):
    half = HD // 2
    rolled = jnp.concatenate([-values[..., half:], values[..., :half]], axis=-1)
    return values * cosine + rolled * sine


def unrotate(grads, cosine, sine):
    half = HD // 2
    turned = grads * sine
    return grads * cosine + jnp.concatenate([turned[..., half:], -turned[..., :half]], axis=-1)


def row_positions(deal, rows, block):
    owner = rows // (2 * block)
    local = rows % (2 * block)
    table = jnp.arange(deal.shape[0], dtype=jnp.int32)
    pair = jnp.sum(jnp.where(owner[:, None] == table[None, :], deal[None, :], 0), axis=1)
    return jnp.where(
        local < block, pair * block + local, (2 * deal.shape[0] - 1 - pair) * block + local - block
    )


def swap(value, axis, count, k):
    return lax.ppermute(value, axis, [(i, i ^ k) for i in range(count)])


def make_per_device(n_ctx, n_wa):
    def wa_exchange(value):
        return [value] + [swap(value, "wa", n_wa, k) for k in range(1, n_wa)]

    def gather_weight(shard):
        part = shard.shape[0] // n_ctx
        mine = lax.dynamic_slice_in_dim(shard, lax.axis_index("ctx") * part, part, 0)
        over_wa = lax.all_gather(mine, "wa", axis=0, tiled=False)
        over_all = lax.all_gather(over_wa, "ctx", axis=0, tiled=False)
        return over_all.transpose(1, 0, 2, 3).reshape(shard.shape[0] * n_wa, shard.shape[1])

    def per_device(
        tokens,
        cotangent,
        adapter_index,
        deal,
        w_qkv,
        b_qkv,
        w_o,
        w_gu,
        w_down,
        gain_attn,
        gain_mlp,
        a_qkv,
        b_q,
        b_kv,
        a_o,
        lift_o,
        a_gu,
        lift_gu,
        a_down,
        lift_down,
    ):
        rows, width = tokens.shape[1:]
        block = rows // 2
        rank = b_q.shape[1]
        slots = a_qkv.shape[0]
        kvd = b_kv.shape[3]
        heads = width // HD
        kvh = kvd // HD
        group = heads // kvh
        part_ff = w_down.shape[0]
        scale = 1.0 / math.sqrt(HD)
        wa = lax.axis_index("wa")
        ctx = lax.axis_index("ctx")
        chosen = adapter_index[0]

        def picked(table):
            return lax.dynamic_index_in_dim(table, chosen, 0, keepdims=False)

        grad_out_bf = cotangent[0]
        index_all = jnp.concatenate(wa_exchange(adapter_index))
        full_qkv = gather_weight(w_qkv)
        full_o = gather_weight(w_o)
        grads_all = jnp.concatenate(wa_exchange(grad_out_bf), axis=0)

        query_pos = row_positions(deal, ctx * rows + jnp.arange(rows, dtype=jnp.int32), block)
        key_pos = row_positions(deal, jnp.arange(n_ctx * rows, dtype=jnp.int32), block)
        mask = (key_pos[None, :] <= query_pos[:, None])[:, None, None, :]
        cosine, sine = rope_tables(query_pos)
        gain_one = gain_attn.astype(F32)
        gain_two = gain_mlp.astype(F32)
        x = tokens[0].astype(F32)
        s_aqkv, s_bq, s_bkv = picked(a_qkv), picked(b_q), picked(b_kv)
        s_ao, s_lo, s_agu, s_ld = picked(a_o), picked(lift_o), picked(a_gu), picked(lift_down)

        inv1 = inverse_norm(x)
        h1 = (x * inv1 * gain_one).astype(BF16)
        u1 = dot_nt(h1, s_aqkv).astype(BF16)
        extra = jnp.concatenate(
            [
                dot_nn(u1[:, :rank], s_bq),
                dot_nn(u1[:, rank : 2 * rank], s_bkv[0]),
                dot_nn(u1[:, 2 * rank :], s_bkv[1]),
            ],
            axis=1,
        )
        lin = dot_nn(h1, full_qkv) + b_qkv.astype(F32) + ADAPTER_SCALE * extra
        queries = rotate(lin[:, :width].reshape(rows, heads, HD), cosine, sine)
        queries = queries.astype(BF16).reshape(rows, kvh, group, HD)
        keys = rotate(lin[:, width : width + kvd].reshape(rows, kvh, HD), cosine, sine)
        kv_mine = jnp.concatenate([keys.reshape(rows, kvd), lin[:, width + kvd :]], axis=1)
        kv_all = lax.all_gather(kv_mine.astype(BF16), "ctx", axis=0, tiled=True)
        k_all = kv_all[:, :kvd].reshape(-1, kvh, HD)
        v_all = kv_all[:, kvd:].reshape(-1, kvh, HD)
        scores = jnp.einsum("tkgd,nkd->tkgn", queries, k_all, preferred_element_type=F32) * scale
        scores = jnp.where(mask, scores, MASKED)
        top = jnp.max(scores, axis=-1, keepdims=True)
        expo = jnp.exp(scores - top)
        total = jnp.sum(expo, axis=-1, keepdims=True)
        probs = expo / total
        probs_bf = probs.astype(BF16)
        attn = jnp.einsum("tkgn,nkd->tkgd", probs_bf, v_all, preferred_element_type=F32)
        ob = attn.reshape(rows, width).astype(BF16)
        uo = dot_nt(ob, s_ao).astype(BF16)
        x1 = x + dot_nn(ob, full_o) + ADAPTER_SCALE * dot_nn(uo, s_lo)
        inv2 = inverse_norm(x1)
        h2 = (x1 * inv2 * gain_two).astype(BF16)

        h2_all = jnp.concatenate(wa_exchange(h2), axis=0)
        row_index = jnp.repeat(index_all, rows)[:, None]

        def own_slot(values, wide):
            lane = lax.broadcasted_iota(jnp.int32, (1, values.shape[1]), 1)
            return jnp.where(lane // wide == row_index, values, 0.0).astype(BF16)

        first = wa * part_ff
        lift_g = lax.dynamic_slice_in_dim(lift_gu[:, 0], first, part_ff, 2).reshape(-1, part_ff)
        lift_u = lax.dynamic_slice_in_dim(lift_gu[:, 1], first, part_ff, 2).reshape(-1, part_ff)
        down_a = lax.dynamic_slice_in_dim(a_down, first, part_ff, 2).reshape(-1, part_ff)
        ug_g = own_slot(dot_nt(h2_all, a_gu[:, :rank].reshape(-1, width)), rank)
        ug_u = own_slot(dot_nt(h2_all, a_gu[:, rank:].reshape(-1, width)), rank)
        gate = dot_nn(h2_all, w_gu[0]) + ADAPTER_SCALE * dot_nn(ug_g, lift_g)
        up = dot_nn(h2_all, w_gu[1]) + ADAPTER_SCALE * dot_nn(ug_u, lift_u)
        sigma = jax.nn.sigmoid(gate)
        swish = gate * sigma
        hidden = (swish * up).astype(BF16)
        dud = own_slot(
            ADAPTER_SCALE * dot_nt(grads_all, lift_down.reshape(-1, width)), rank
        )
        g_adown = dot_tn(dud, hidden)
        d_hidden = dot_nt(grads_all, w_down) + dot_nn(dud, down_a)
        d_gate = (d_hidden * up * (sigma * (1.0 + gate * (1.0 - sigma)))).astype(BF16)
        d_up = (d_hidden * swish).astype(BF16)
        g_bgu = ADAPTER_SCALE * jnp.stack([dot_tn(ug_g, d_gate), dot_tn(ug_u, d_up)])
        out_part = dot_nn(hidden, w_down).astype(BF16)
        ud_part = dot_nt(hidden, down_a)
        d_h2_part = (dot_nt(d_gate, w_gu[0]) + dot_nt(d_up, w_gu[1])).astype(BF16)
        dug_g = ADAPTER_SCALE * dot_nt(d_gate, lift_g)
        dug_u = ADAPTER_SCALE * dot_nt(d_up, lift_u)

        def own_columns(values, k):
            mine = values[k * rows : (k + 1) * rows].reshape(rows, slots, rank)
            hot = (jnp.arange(slots) == index_all[k])[None, :, None]
            return jnp.sum(jnp.where(hot, mine, 0.0), axis=1)

        def wa_collect(parts):
            total = parts[0].astype(F32)
            for k in range(1, n_wa):
                total = total + swap(parts[k], "wa", n_wa, k).astype(F32)
            return total

        d_h2_sent = [d_h2_part[k * rows : (k + 1) * rows] for k in range(n_wa)]
        small_sent = [
            jnp.concatenate(
                [own_columns(dug_g, k), own_columns(dug_u, k), own_columns(ud_part, k)], axis=1
            )
            for k in range(n_wa)
        ]
        small = wa_collect(small_sent).astype(BF16)
        dug, ud = small[:, : 2 * rank], small[:, 2 * rank :]
        d_h2 = wa_collect(d_h2_sent) + dot_nn(dug, s_agu)
        out = (
            x1
            + wa_collect([out_part[k * rows : (k + 1) * rows] for k in range(n_wa)])
            + ADAPTER_SCALE * dot_nn(ud, s_ld)
        ).astype(BF16)
        g_ld = ADAPTER_SCALE * dot_tn(ud, grad_out_bf)
        g_agu = dot_tn(dug, h2)

        d_x1 = grad_out_bf.astype(F32) + norm_pull(x1, inv2, gain_two, d_h2)
        go = d_x1.astype(BF16)
        duo = (ADAPTER_SCALE * dot_nt(go, s_lo)).astype(BF16)
        g_lo = ADAPTER_SCALE * dot_tn(uo, go)
        g_ao = dot_tn(duo, ob)
        dob = (dot_nt(go, full_o) + dot_nn(duo, s_ao)).astype(BF16).reshape(rows, kvh, group, HD)
        delta = jnp.sum(dob.astype(F32) * attn, axis=-1, keepdims=True)
        d_values = jnp.einsum("tkgn,tkgd->nkd", probs_bf, dob, preferred_element_type=F32)
        d_probs = jnp.einsum("tkgd,nkd->tkgn", dob, v_all, preferred_element_type=F32)
        ds = (probs * (d_probs - delta)).astype(BF16)
        d_query = jnp.einsum("tkgn,nkd->tkgd", ds, k_all, preferred_element_type=F32) * scale
        d_keys = jnp.einsum("tkgn,tkgd->nkd", ds, queries, preferred_element_type=F32) * scale
        d_kv_part = jnp.concatenate([d_keys.reshape(-1, kvd), d_values.reshape(-1, kvd)], axis=1)
        d_kv = lax.all_to_all(d_kv_part.astype(BF16), "ctx", 0, 0, tiled=True)
        d_kv = jnp.sum(d_kv.reshape(n_ctx, rows, 2 * kvd).astype(F32), axis=0)
        d_q_lin = unrotate(d_query.reshape(rows, heads, HD), cosine, sine).reshape(rows, width)
        d_k_lin = unrotate(d_kv[:, :kvd].reshape(rows, kvh, HD), cosine, sine).reshape(rows, kvd)
        d_lin = jnp.concatenate([d_q_lin, d_k_lin, d_kv[:, kvd:]], axis=1).astype(BF16)
        dl_q, dl_k, dl_v = d_lin[:, :width], d_lin[:, width : width + kvd], d_lin[:, width + kvd :]
        du1 = (
            ADAPTER_SCALE
            * jnp.concatenate(
                [dot_nt(dl_q, s_bq), dot_nt(dl_k, s_bkv[0]), dot_nt(dl_v, s_bkv[1])], axis=1
            )
        ).astype(BF16)
        g_bq = ADAPTER_SCALE * dot_tn(u1[:, :rank], dl_q)
        g_bk = ADAPTER_SCALE * dot_tn(u1[:, rank : 2 * rank], dl_k)
        g_bv = ADAPTER_SCALE * dot_tn(u1[:, 2 * rank :], dl_v)
        g_aqkv = dot_tn(du1, h1)
        d_h1 = dot_nt(d_lin, full_qkv) + dot_nn(du1, s_aqkv)
        grad_x = d_x1 + norm_pull(x, inv1, gain_one, d_h1)

        def reduce_share(flat):
            count = flat.shape[0]
            padded = -(-count // (n_ctx * 1024)) * n_ctx * 1024
            flat = jnp.pad(flat, (0, padded - count)).reshape(n_ctx, -1, 128).astype(BF16)
            got = lax.all_to_all(flat, "ctx", 0, 0, tiled=True)
            return jnp.sum(got.astype(F32), axis=0).astype(BF16)

        def share_all(share, count):
            over_wa = lax.all_gather(share, "wa", axis=0, tiled=False)
            got = lax.all_gather(over_wa, "ctx", axis=0, tiled=False)
            return got.transpose(1, 0, 2, 3).reshape(n_wa, -1)[:, :count]

        ff_flat = jnp.concatenate(
            [g_bgu.reshape(2, slots, rank, part_ff).transpose(1, 0, 2, 3).ravel(), g_adown.ravel()]
        )
        seq_parts = [g_aqkv, g_bq, g_bk, g_bv, g_ao, g_lo, g_agu, g_ld]
        seq_flat = jnp.concatenate([part.ravel() for part in seq_parts])
        ff_all = share_all(reduce_share(ff_flat), ff_flat.shape[0])
        seq_all = share_all(reduce_share(seq_flat), seq_flat.shape[0])
        cut = slots * 2 * rank * part_ff
        r_bgu = ff_all[:, :cut].reshape(n_wa, slots, 2, rank, part_ff).astype(F32)
        r_bgu = r_bgu.transpose(1, 2, 3, 0, 4).reshape(slots, 2, rank, n_wa * part_ff)
        r_ad = ff_all[:, cut:].reshape(n_wa, slots, rank, part_ff).astype(F32)
        r_ad = r_ad.transpose(1, 2, 0, 3).reshape(slots, rank, n_wa * part_ff)
        own = lax.dynamic_update_slice(jnp.zeros((n_wa,), jnp.int32), adapter_index, (wa,))
        for k in range(1, n_wa):
            own = lax.dynamic_update_slice(own, index_all[k : k + 1], (wa ^ k,))
        hot = (own[None, :] == jnp.arange(slots)[:, None]).astype(F32)
        by_slot = jnp.sum(hot[:, :, None] * seq_all[None].astype(F32), axis=1)
        results = []
        at = 0
        for part in seq_parts:
            results.append(by_slot[:, at : at + part.size].reshape((slots,) + part.shape))
            at += part.size
        r_aqkv, r_bq, r_bk, r_bv, r_ao, r_lo, r_agu, r_ld = results
        return (
            out[None],
            grad_x[None],
            r_aqkv,
            r_bq,
            jnp.stack([r_bk, r_bv], axis=1),
            r_ao,
            r_lo,
            r_agu,
            r_bgu,
            r_ad,
            r_ld,
        )

    return per_device


def solution(mesh):
    rep = P()
    return jax.shard_map(
        make_per_device(mesh.shape["ctx"], mesh.shape["wa"]),
        mesh=mesh,
        in_specs=(
            P("wa", "ctx", None),
            P("wa", "ctx", None),
            P("wa"),
            rep,
            P("wa", None),
            rep,
            P("wa", None),
            P(None, None, "wa"),
            P("wa", None),
        )
        + (rep,) * 11,
        out_specs=(P("wa", "ctx", None), P("wa", "ctx", None)) + (rep,) * 9,
        check_vma=False,
    )
```

time: 2040 us -> 543 us (0.27)
  waiting for transfers between devices: 1760 us -> 134 us
  blocking collectives: 0 us -> 80.4 us
  local copies, waits for them, and re-layouts: 44.7 us -> 115 us
  matrix products: 168 us -> 104 us
  starting transfers between devices: 0.27 us -> 43.2 us
    all_gather x5, waiting for transfers between devices: 1530 us -> 53.9 us  [the longest x2 33.3 us: gather_weight(): over_all = lax.all_gather(over_wa, 'ctx', axis=0, tiled=False)]
    psum x1 -> x0, waiting for transfers between devices: 205 us -> none  [per_device(): lax.psum((spread(grad_aqkv), spread(query_bias_gradient), spread(key_valu...]
    all_gather x0 -> x4, blocking collectives: none -> 80.4 us  [the longest x2 41.7 us: share_all(): over_wa = lax.all_gather(share, 'wa', axis=0, tiled=False)]
    ppermute x0 -> x18, waiting for transfers between devices: none -> 69.1 us  [swap(): return lax.ppermute(value, axis, [(i, i ^ k) for i in range(count)])]
    dot_general x57 -> x49, matrix products: 168 us -> 99.3 us  [the longest x16 41.9 us: dot_nn(): lax.dot_general(a, b, (((1,), (0,)), ((), ())), preferred_element_type=F32)]
    reshape x2 -> x19, local copies, waits for them, and re-layouts: 0.14 us -> 44.2 us  [the longest x3 21.7 us: per_device(): r_bgu.transpose(1, 2, 3, 0, 4).reshape(slots, 2, rank, n_wa * part_ff)]
    ppermute x0 -> x18, starting transfers between devices: none -> 31.6 us  [swap(): return lax.ppermute(value, axis, [(i, i ^ k) for i in range(count)])]
    reduce_scatter x1 -> x0, waiting for transfers between devices: 30.2 us -> none  [per_device(): lax.psum_scatter(d_kv_all.astype(jnp.bfloat16), 'ctx', scatter_dimension=...]
  transfers between devices with their start and end apart: 7 -> 26, of which waited for: 7 -> 11; matrix products, arithmetic and copies ran while one was open for 5% -> 23% of each run, Pallas kernels for 0% -> 0%
where the time goes in v1:
time: 543 us; the launch traced here: 536 us
  waiting for transfers between devices  134 us (25%)
  local copies, waits for them, and re-layouts  115 us (21%)
  matrix products  104 us (19%)
  blocking collectives  80.4 us (15%)
  starting transfers between devices  43.2 us (8%)
  other arithmetic  43.2 us (8%)
  between operations  16.5 us (3%)
    ppermute x18, waiting for transfers between devices, swap(): return lax.ppermute(value, axis, [(i, i ^ k) for i in range(count)])  69.1 us
    unnamed x166, local copies, waits for them, and re-layouts  44.3 us
    dot_general x16, matrix products, dot_nn(): lax.dot_general(a, b, (((1,), (0,)), ((), ())), preferred_element_type=F32)  41.9 us
    all_gather x2, blocking collectives, share_all(): over_wa = lax.all_gather(share, 'wa', axis=0, tiled=False)  41.7 us
    all_gather x2, blocking collectives, gather_weight(): over_wa = lax.all_gather(mine, 'wa', axis=0, tiled=False)  38.7 us
    dot_general x17, matrix products, dot_nt(): lax.dot_general(a, b, (((1,), (1,)), ((), ())), preferred_element_type=F32)  38.7 us
    all_gather x2, waiting for transfers between devices, gather_weight(): over_all = lax.all_gather(over_wa, 'ctx', axis=0, tiled=False)  33.3 us
    ppermute x18, starting transfers between devices, swap(): return lax.ppermute(value, axis, [(i, i ^ k) for i in range(count)])  31.6 us
  transfers between devices with their start and end apart: 26, of which 11 were waited for; matrix products, arithmetic and copies ran while one was open for 23% of the time, Pallas kernels for 0%

profile of v1, /device:TPU:0, one launch (start us, length us, event | category | flops | bytes accessed | tf_op | source)
XLA Modules:
  0.0 536.3 jit_solution(5459884633676702977)
XLA Ops:
  8.6 21.7 %all-gather = bf16[192,2048]{1,0:T(8,128)(2,1)} all-gather(bf16[48,2048]{1,0:T(8,128)(2,1)S(1)} %constant_dynamic-slice_fusion.4), channel_id=2, replica_groups=mesh['ctx'=8,'wa'=4] {'wa'}, dimensions={0}, use_global_device_ids=true | all-gather | bytes 983040 | tf_op jit(solution)/shard_map/all_gather | solution.py:80
  31.3 17.0 %all-gather.2 = bf16[192,1536]{1,0:T(8,128)(2,1)} all-gather(bf16[48,1536]{1,0:T(8,128)(2,1)S(1)} %constant_dynamic-slice_fusion.3), channel_id=4, replica_groups=mesh['ctx'=8,'wa'=4] {'wa'}, dimensions={0}, use_global_device_ids=true | all-gather | bytes 737280 | tf_op jit(solution)/shard_map/all_gather | solution.py:80
  48.5 2.3 collective-permute-start.4
  50.8 2.1 collective-permute-start.5
  66.7 9.0 %all-gather.16.cloned.1.call-done = bf16[32,48,2048]{2,1,0:T(8,128)(2,1)} async-done(((bf16[4,48,2048]{2,1,0:T(8,128)(2,1)}), bf16[32,48,2048]{2,1,0:T(8,128)(2,1)}) %all-gather.16.cloned.1.call-update) | async-done | bytes 6291472 | tf_op jit(solution)/shard_map/all_gather | solution.py:81
  75.7 3.4 copy.121
  92.2 24.4 %all-gather.18.cloned.1.call-done = bf16[32,48,1536]{2,1,0:T(8,128)(2,1)} async-done(((bf16[4,48,1536]{2,1,0:T(8,128)(2,1)}), bf16[32,48,1536]{2,1,0:T(8,128)(2,1)}) %all-gather.18.cloned.1.call-update) | async-done | bytes 4718608 | tf_op jit(solution)/shard_map/all_gather | solution.py:81
  116.5 4.8 copy.130
  122.0 20.6 %all-gather.14.cloned.1.call-done = bf16[1024,512]{1,0:T(8,128)(2,1)} async-done(((bf16[128,512]{1,0:T(8,128)(2,1)}), bf16[1024,512]{1,0:T(8,128)(2,1)}) %all-gather.14.cloned.1.call-update) | async-done | bytes 1048592 | tf_op jit(solution)/shard_map/all_gather | solution.py:155
  144.7 4.9 fusion.183
  149.6 3.6 fusion.32
  159.5 2.4 collective-permute-start.1
  165.3 11.9 %collective-permute-done = bf16[128,1536]{1,0:T(8,128)(2,1)S(1)} collective-permute-done((bf16[128,1536]{1,0:T(8,128)(2,1)S(1)}, bf16[128,1536]{1,0:T(8,128)(2,1)S(1)}, u32[]{:S(2)}, u32[]{:S(2)}) %collective-permute-start) | collective-permute-done | bytes 393248 | tf_op jit(solution)/shard_map/ppermute | solution.py:70
  177.2 12.1 %collective-permute-done.1 = bf16[128,1536]{1,0:T(8,128)(2,1)S(1)} collective-permute-done((bf16[128,1536]{1,0:T(8,128)(2,1)S(1)}, bf16[128,1536]{1,0:T(8,128)(2,1)S(1)}, u32[]{:S(2)}, u32[]{:S(2)}) %collective-permute-start.1) | collective-permute-done | bytes 393248 | tf_op jit(solution)/shard_map/ppermute | solution.py:70
  192.5 9.1 %fusion.18 = f32[512,2240]{0,1:T(8,128)} fusion(f32[512,2240]{0,1:T(8,128)S(1)} %convolution_multiply_fusion, bf16[2,1536,2240]{1,2,0:T(8,128)(2,1)} %param.27, bf16[128,1536]{1,0:T(8,128)(2,1)S(1)} %collective-permute-done.2, bf16[128,1536]{1,0:T(8,128)(2,1)S(1)} %collective-permute-done.1, bf16[128,1536]{1,0:T(8,128)(2,1)S(1)} %collective-permute-done, ...), kind=kOutput, calls=%fused_computation.22 | convolution fusion | flops 3530653696 | bytes 17629184 | tf_op jit(solution)/shard_map/dot_general | solution.py:18
  201.6 9.3 %fusion.15 = f32[512,2240]{0,1:T(8,128)} fusion(f32[512,2240]{0,1:T(8,128)S(1)} %convolution_multiply_fusion.1, bf16[2,1536,2240]{1,2,0:T(8,128)(2,1)} %param.27, bf16[128,1536]{1,0:T(8,128)(2,1)S(1)} %collective-permute-done.2, bf16[128,1536]{1,0:T(8,128)(2,1)S(1)} %collective-permute-done.1, bf16[128,1536]{1,0:T(8,128)(2,1)S(1)} %collective-permute-done, ...), kind=kOutput, calls=%fused_computation.21 | convolution fusion | flops 3530653696 | bytes 17629184 | tf_op jit(solution)/shard_map/dot_general | solution.py:18
  210.9 10.6 %multiply_convert_fusion = (bf16[512,2240]{0,1:T(8,128)(2,1)S(1)}, bf16[512,2240]{0,1:T(8,128)(2,1)S(1)}, bf16[512,2240]{0,1:T(8,128)(2,1)S(1)}) fusion(f32[512,2240]{0,1:T(8,128)} %fusion.15, f32[512,2240]{0,1:T(8,128)} %fusion.18, f32[512,2240]{0,1:T(8,128)S(1)} %fusion.187, bf16[2240,1536]{1,0:T(8,128)(2,1)} %param.28, ...), kind=kOutput, calls=%fused_computation.25 | convolution fusion | flops 3547856896 | bytes 29097984 | tf_op jit(solution)/shard_map/dot_general | solution.py:26
  225.9 6.8 %fusion.1 = f32[512,1536]{1,0:T(8,128)S(1)} fusion(bf16[512,2240]{0,1:T(8,128)(2,1)S(1)} %get-tuple-element.25, bf16[2,1536,2240]{1,2,0:T(8,128)(2,1)} %param.27), kind=kOutput, calls=%fused_computation.2 | convolution fusion | flops 3523215360 | bytes 12320768 | tf_op jit(solution)/shard_map/dot_general | solution.py:26
  233.5 8.1 %collective-permute-start.12 = (f32[128,48]{0,1:T(8,128)S(1)}, f32[128,48]{0,1:T(8,128)S(1)}, u32[]{:S(2)}, u32[]{:S(2)}) collective-permute-start(f32[128,48]{0,1:T(8,128)S(1)} %pad_maximum_fusion.11), channel_id=1, source_target_pairs={{0,1},{1,0},{2,3},{3,2},{4,5},{5,4},{6,7},{7,6},{8,9},{9,8},{10,11... | collective-permute-start | bytes 73736 | tf_op jit(solution)/shard_map/ppermute | solution.py:70
  244.3 4.1 fusion.29
  259.1 7.1 %collective-permute-done.15 = bf16[128,1536]{1,0:T(8,128)(2,1)S(1)} collective-permute-done((bf16[128,1536]{1,0:T(8,128)(2,1)}, bf16[128,1536]{1,0:T(8,128)(2,1)S(1)}, u32[]{:S(2)}, u32[]{:S(2)}) %collective-permute-start.15) | collective-permute-done | bytes 393248 | tf_op jit(solution)/shard_map/ppermute | solution.py:70
  266.2 14.5 %collective-permute-done.16 = bf16[128,1536]{1,0:T(8,128)(2,1)} collective-permute-done((bf16[128,1536]{1,0:T(8,128)(2,1)}, bf16[128,1536]{1,0:T(8,128)(2,1)}, u32[]{:S(2)}, u32[]{:S(2)}) %collective-permute-start.16) | collective-permute-done | bytes 393248 | tf_op jit(solution)/shard_map/ppermute | solution.py:70
  290.4 4.1 fusion.10
  301.0 4.4 all-to-all-start
  311.0 9.8 %all-to-all-done = bf16[8,128,512]{1,2,0:T(8,128)(2,1)} async-done(((bf16[8,128,512]{1,2,0:T(8,128)(2,1)}), bf16[8,128,512]{1,2,0:T(8,128)(2,1)}, u32[]{:S(2)}, u32[]{:S(2)}) %all-to-all-start) | async-done | bytes 1048608 | tf_op jit(solution)/shard_map/all_to_all | solution.py:246
  330.0 3.5 all-to-all-start.1
  336.3 3.2 convolution_convert_fusion
  339.5 2.0 reshape.615
  342.5 19.3 %all-gather.4 = bf16[896,128]{1,0:T(8,128)(2,1)} all-gather(bf16[224,128]{1,0:T(8,128)(2,1)S(1)} %reduce_sum.243), channel_id=6, replica_groups=mesh['ctx'=8,'wa'=4] {'wa'}, dimensions={0}, use_global_device_ids=true | all-gather | bytes 286720 | tf_op jit(solution)/shard_map/all_gather | solution.py:273
  363.8 3.6 all-to-all-start.2
  367.4 7.6 %convolution_convert_fusion.1 = bf16[512,1536]{1,0:T(8,128)(2,1)S(1)} fusion(bf16[512,2240]{0,1:T(8,128)(2,1)} %copy-done.7, bf16[2240,1536]{1,0:T(8,128)(2,1)} %param.28), kind=kOutput, calls=%fused_computation.39 | convolution fusion | flops 3524001792 | bytes 10747904 | tf_op jit(solution)/shard_map/dot_general | solution.py:18
  379.2 2.4 collective-permute-start.8
  383.8 12.9 %collective-permute-done.6 = bf16[128,1536]{1,0:T(8,128)(2,1)} collective-permute-done((bf16[128,1536]{1,0:T(8,128)(2,1)}, bf16[128,1536]{1,0:T(8,128)(2,1)}, u32[]{:S(2)}, u32[]{:S(2)}) %collective-permute-start.6) | collective-permute-done | bytes 393248 | tf_op jit(solution)/shard_map/ppermute | solution.py:70
  396.7 10.5 %collective-permute-done.7 = bf16[128,1536]{1,0:T(8,128)(2,1)} collective-permute-done((bf16[128,1536]{1,0:T(8,128)(2,1)}, bf16[128,1536]{1,0:T(8,128)(2,1)}, u32[]{:S(2)}, u32[]{:S(2)}) %collective-permute-start.7) | collective-permute-done | bytes 393248 | tf_op jit(solution)/shard_map/ppermute | solution.py:70
  407.2 2.5 fusion.85
  409.9 22.4 %all-gather.6 = bf16[1696,128]{1,0:T(8,128)(2,1)} all-gather(bf16[424,128]{1,0:T(8,128)(2,1)S(1)} %reduce_sum.245), channel_id=8, replica_groups=mesh['ctx'=8,'wa'=4] {'wa'}, dimensions={0}, use_global_device_ids=true | all-gather | bytes 542720 | tf_op jit(solution)/shard_map/all_gather | solution.py:273
  433.4 5.0 fusion.77
  443.2 7.8 %copy.210 = f32[1,4,1792,128]{3,1,2,0:T(4,128)S(1)} copy(f32[1,4,1792,128]{3,2,1,0:T(8,128)S(1)} %bitcast.369) | data formatting | bytes 7340032
  451.0 10.5 %multiply_reduce_fusion = f32[4,229376]{1,0:T(4,128)S(1)} fusion(f32[4,229376]{1,0:T(4,128)S(1)} %bitcast.370, f32[4,4]{1,0:T(4,128)S(1)} %fusion.157), kind=kLoop, calls=%fused_computation.1 | loop fusion | flops 6422528 | bytes 7340096 | tf_op jit(solution)/shard_map/reduce_sum | solution.py:293
  469.2 2.2 copy.148
  471.4 18.5 %copy.211 = bf16[1,4,3392,128]{3,1,2,0:T(4,128)(2,1)S(1)} copy(bf16[1,4,3392,128]{3,2,1,0:T(8,128)(2,1)S(1)} %bitcast.372) | data formatting | bytes 6946816
  489.9 2.6 slice_convert_fusion
  494.3 7.5 %reshape.631 = f32[4,4,2,16,2240]{4,3,2,1,0:T(8,128)} reshape(f32[4,286720]{1,0:T(4,128)} %slice_convert_fusion) | data formatting | bytes 9175040 | tf_op jit(solution)/shard_map/reshape | solution.py:286
  501.8 7.6 %copy.149 = f32[4,2,16,4,2240]{4,3,2,1,0:T(4,128)} copy(f32[4,2,16,4,2240]{4,2,1,0,3:T(8,128)} %bitcast.368) | data formatting | bytes 9175040 | tf_op jit(solution)/shard_map/reshape | solution.py:286
  509.4 6.7 %reshape.625 = f32[4,2,16,8960]{3,2,1,0:T(8,128)} reshape(f32[4,2,16,4,2240]{4,3,2,1,0:T(4,128)} %copy.149) | data formatting | bytes 9175040 | tf_op jit(solution)/shard_map/reshape | solution.py:286
  516.0 4.5 reshape.633
  520.6 4.7 copy.150
  525.3 4.0 reshape.627
  (356 shorter events, 120.2 us)
Async XLA Ops:
  7.2 48.1 %copy-start.52 = (bf16[1536]{0:T(1024)(128)(2,1)S(1)}, bf16[1536]{0:T(1024)(128)(2,1)}, u32[]{:S(2)}) copy-start(bf16[1536]{0:T(1024)(128)(2,1)} %param.29) | copy-start | bytes 9220
  7.2 48.1 %copy-start.53 = (bf16[2048]{0:T(1024)(128)(2,1)S(1)}, bf16[2048]{0:T(1024)(128)(2,1)}, u32[]{:S(2)}) copy-start(bf16[2048]{0:T(1024)(128)(2,1)} %param.25) | copy-start | bytes 12292
  7.2 48.1 %copy-start.61 = (s32[8]{0:T(128)S(1)}, s32[8]{0:T(128)}, u32[]{:S(2)}) copy-start(s32[8]{0:T(128)} %param.23) | copy-start | bytes 100
  7.2 48.7 %copy-start.54 = (bf16[1536]{0:T(1024)(128)(2,1)S(1)}, bf16[1536]{0:T(1024)(128)(2,1)}, u32[]{:S(2)}) copy-start(bf16[1536]{0:T(1024)(128)(2,1)} %param.30) | copy-start | bytes 9220
  7.2 50.0 %copy-start.6 = (bf16[1,128,1536]{2,1,0:T(8,128)(2,1)S(1)}, bf16[1,128,1536]{2,1,0:T(8,128)(2,1)}, u32[]{:S(2)}) copy-start(bf16[1,128,1536]{2,1,0:T(8,128)(2,1)} %param.20) | copy-start | bytes 1179652
  7.2 68.5 %all-gather.16.cloned.1.call-start = ((), (), s32[]{:S(2)}) async-start(), calls=%async_computation.4 | async-start | bytes 7077888 | tf_op jit(solution)/shard_map/all_gather | solution.py:81
  30.4 86.2 %all-gather.18.cloned.1.call-start = ((), (), s32[]{:S(2)}) async-start(), calls=%async_computation.5 | async-start | bytes 5308416 | tf_op jit(solution)/shard_map/all_gather | solution.py:81
  48.4 94.2 %all-gather.14.cloned.1.call-start = ((), (), s32[]{:S(2)}) async-start(), calls=%async_computation.3 | async-start | bytes 1179648 | tf_op jit(solution)/shard_map/all_gather | solution.py:155
  48.4 36.2 %collective-permute-start.3 = (s32[1]{0:T(128)}, s32[1]{0:T(128)}, u32[]{:S(2)}, u32[]{:S(2)}) collective-permute-start(s32[1]{0:T(128)} %param.22), channel_id=1, source_target_pairs={{0,1},{1,0},{2,3},{3,2},{4,5},{5,4},{6,7},{7,6},{8,9},{9,8},{10,11... | collective-permute-start | bytes 20 | tf_op jit(solution)/shard_map/ppermute | solution.py:70
  48.5 38.8 %collective-permute-start.4 = (s32[1]{0:T(128)}, s32[1]{0:T(128)}, u32[]{:S(2)}, u32[]{:S(2)}) collective-permute-start(s32[1]{0:T(128)} %param.22), channel_id=1, source_target_pairs={{0,2},{1,3},{2,0},{3,1},{4,6},{5,7},{6,4},{7,5},{8,10},{9,11},{10,... | collective-permute-start | bytes 20 | tf_op jit(solution)/shard_map/ppermute | solution.py:70
  50.8 37.7 %collective-permute-start.5 = (s32[1]{0:T(128)}, s32[1]{0:T(128)}, u32[]{:S(2)}, u32[]{:S(2)}) collective-permute-start(s32[1]{0:T(128)} %param.22), channel_id=1, source_target_pairs={{0,3},{1,2},{2,1},{3,0},{4,7},{5,6},{6,5},{7,4},{8,11},{9,10},{10,... | collective-permute-start | bytes 20 | tf_op jit(solution)/shard_map/ppermute | solution.py:70
  52.9 109.0 %collective-permute-start.10 = (bf16[128,1536]{1,0:T(8,128)(2,1)}, bf16[128,1536]{1,0:T(8,128)(2,1)}, u32[]{:S(2)}, u32[]{:S(2)}) collective-permute-start(bf16[128,1536]{1,0:T(8,128)(2,1)} %bitcast.33), channel_id=1, source_target_pairs={{0,2},{1,3},{2,0},{3,1},{4,6},{5,7},{6,4},{7,5},{8,10},{9,11},{10,... | collective-permute-start | bytes 1179656 | tf_op jit(solution)/shard_map/ppermute | solution.py:70
  52.9 109.5 %collective-permute-start.11 = (bf16[128,1536]{1,0:T(8,128)(2,1)}, bf16[128,1536]{1,0:T(8,128)(2,1)}, u32[]{:S(2)}, u32[]{:S(2)}) collective-permute-start(bf16[128,1536]{1,0:T(8,128)(2,1)} %bitcast.33), channel_id=1, source_target_pairs={{0,3},{1,2},{2,1},{3,0},{4,7},{5,6},{6,5},{7,4},{8,11},{9,10},{10,... | collective-permute-start | bytes 1179656 | tf_op jit(solution)/shard_map/ppermute | solution.py:70
  55.8 26.3 %copy-start.28 = (f32[128,128]{1,0:T(8,128)}, f32[128,128]{1,0:T(8,128)S(1)}, u32[]{:S(2)}) copy-start(f32[128,128]{1,0:T(8,128)S(1)} %copy.123) | copy-start | bytes 196612
  57.9 21.2 %copy-start.49 = (f32[128]{0:T(128)}, f32[128]{0:T(128)S(1)}, u32[]{:S(2)}) copy-start(f32[128]{0:T(128)S(1)} %get-tuple-element.69) | copy-start | bytes 1540
  84.7 77.8 %collective-permute-start.9 = (bf16[128,1536]{1,0:T(8,128)(2,1)}, bf16[128,1536]{1,0:T(8,128)(2,1)}, u32[]{:S(2)}, u32[]{:S(2)}) collective-permute-start(bf16[128,1536]{1,0:T(8,128)(2,1)} %bitcast.33), channel_id=1, source_target_pairs={{0,1},{1,0},{2,3},{3,2},{4,5},{5,4},{6,7},{7,6},{8,9},{9,8},{10,11... | collective-permute-start | bytes 1179656 | tf_op jit(solution)/shard_map/ppermute | solution.py:70
  121.9 27.7 %copy-start.22 = (bf16[128,2,6,128]{0,3,2,1:T(8,128)(2,1)}, bf16[128,2,6,128]{0,3,2,1:T(8,128)(2,1)S(1)}, u32[]{:S(2)}) copy-start(bf16[128,2,6,128]{0,3,2,1:T(8,128)(2,1)S(1)} %fusion.71) | copy-start | bytes 1179652
  121.9 22.7 %copy-start.36 = (pred[128,1024]{0,1:T(8,128)(4,1)S(1)}, pred[128,1024]{0,1:T(8,128)(4,1)}, u32[]{:S(2)}) copy-start(pred[128,1024]{0,1:T(8,128)(4,1)} %broadcast_compare_fusion) | copy-start | bytes 393220
  157.9 43.6 %copy-start.20 = (bf16[128,1536]{1,0:T(8,128)(2,1)}, bf16[128,1536]{1,0:T(8,128)(2,1)S(1)}, u32[]{:S(2)}) copy-start(bf16[128,1536]{1,0:T(8,128)(2,1)S(1)} %multiply_convert_fusion.3) | copy-start | bytes 1179652
  158.0 19.2 %collective-permute-start = (bf16[128,1536]{1,0:T(8,128)(2,1)S(1)}, bf16[128,1536]{1,0:T(8,128)(2,1)S(1)}, u32[]{:S(2)}, u32[]{:S(2)}) collective-permute-start(bf16[128,1536]{1,0:T(8,128)(2,1)S(1)} %multiply_convert_fusion.3), channel_id=1, source_target_pairs={{0,1},{1,0},{2,3},{3,2},{4,5},{5,4},{6,7},{7,6},{8,9},{9,8},{10,11... | collective-permute-start | bytes 1179656 | tf_op jit(solution)/shard_map/ppermute | solution.py:70
  159.5 29.8 %collective-permute-start.1 = (bf16[128,1536]{1,0:T(8,128)(2,1)S(1)}, bf16[128,1536]{1,0:T(8,128)(2,1)S(1)}, u32[]{:S(2)}, u32[]{:S(2)}) collective-permute-start(bf16[128,1536]{1,0:T(8,128)(2,1)S(1)} %multiply_convert_fusion.3), channel_id=1, source_target_pairs={{0,2},{1,3},{2,0},{3,1},{4,6},{5,7},{6,4},{7,5},{8,10},{9,11},{10,... | collective-permute-start | bytes 1179656 | tf_op jit(solution)/shard_map/ppermute | solution.py:70
  161.9 27.4 %collective-permute-start.2 = (bf16[128,1536]{1,0:T(8,128)(2,1)S(1)}, bf16[128,1536]{1,0:T(8,128)(2,1)S(1)}, u32[]{:S(2)}, u32[]{:S(2)}) collective-permute-start(bf16[128,1536]{1,0:T(8,128)(2,1)S(1)} %multiply_convert_fusion.3), channel_id=1, source_target_pairs={{0,3},{1,2},{2,1},{3,0},{4,7},{5,6},{6,5},{7,4},{8,11},{9,10},{10,... | collective-permute-start | bytes 1179656 | tf_op jit(solution)/shard_map/ppermute | solution.py:70
  164.4 24.8 %copy-start.35 = (bf16[4,16,1536]{2,1,0:T(8,128)(2,1)S(1)}, bf16[4,16,1536]{2,1,0:T(8,128)(2,1)}, u32[]{:S(2)}) copy-start(bf16[4,16,1536]{2,1,0:T(8,128)(2,1)} %get-tuple-element.49) | copy-start | bytes 589828
  165.3 24.6 %copy-start.12 = (bf16[4,1,16,2240]{3,2,1,0:T(8,128)(2,1)S(1)}, bf16[4,1,16,2240]{3,2,1,0:T(8,128)(2,1)}, u32[]{:S(2)}) copy-start(bf16[4,1,16,2240]{3,2,1,0:T(8,128)(2,1)} %get-tuple-element.82) | copy-start | bytes 860164
  225.3 19.0 %slice-start.5 = ((s8[13762560]{0:T(1024)(128)(4,1)}), s8[4194304]{0:T(1024)(128)(4,1)S(1)}, s32[]{:S(2)}) async-start(s8[13762560]{0:T(1024)(128)(4,1)} %bitcast.447), calls=%async_computation.13 | async-start | bytes 8388608
  225.8 18.4 %slice-start.6 = ((s8[13762560]{0:T(1024)(128)(4,1)}), s8[4194304]{0:T(1024)(128)(4,1)S(1)}, s32[]{:S(2)}) async-start(s8[13762560]{0:T(1024)(128)(4,1)} %bitcast.447), calls=%async_computation.14 | async-start | bytes 8388608
  225.9 18.4 %slice-start.7 = ((s8[13762560]{0:T(1024)(128)(4,1)}), s8[4194304]{0:T(1024)(128)(4,1)S(1)}, s32[]{:S(2)}) async-start(s8[13762560]{0:T(1024)(128)(4,1)} %bitcast.447), calls=%async_computation.15 | async-start | bytes 8388608
  225.9 18.4 %slice-start.8 = ((s8[13762560]{0:T(1024)(128)(4,1)}), s8[1179648]{0:T(1024)(128)(4,1)S(1)}, s32[]{:S(2)}) async-start(s8[13762560]{0:T(1024)(128)(4,1)} %bitcast.447), calls=%async_computation.16 | async-start | bytes 2359296
  233.5 19.1 %collective-permute-start.12 = (f32[128,48]{0,1:T(8,128)S(1)}, f32[128,48]{0,1:T(8,128)S(1)}, u32[]{:S(2)}, u32[]{:S(2)}) collective-permute-start(f32[128,48]{0,1:T(8,128)S(1)} %pad_maximum_fusion.11), channel_id=1, source_target_pairs={{0,1},{1,0},{2,3},{3,2},{4,5},{5,4},{6,7},{7,6},{8,9},{9,8},{10,11... | collective-permute-start | bytes 73736 | tf_op jit(solution)/shard_map/ppermute | solution.py:70
  241.6 12.4 %collective-permute-start.13 = (f32[128,48]{0,1:T(8,128)S(1)}, f32[128,48]{0,1:T(8,128)S(1)}, u32[]{:S(2)}, u32[]{:S(2)}) collective-permute-start(f32[128,48]{0,1:T(8,128)S(1)} %pad_maximum_fusion.12), channel_id=1, source_target_pairs={{0,2},{1,3},{2,0},{3,1},{4,6},{5,7},{6,4},{7,5},{8,10},{9,11},{10,... | collective-permute-start | bytes 73736 | tf_op jit(solution)/shard_map/ppermute | solution.py:70
  242.8 11.3 %collective-permute-start.14 = (f32[128,48]{0,1:T(8,128)S(1)}, f32[128,48]{0,1:T(8,128)S(1)}, u32[]{:S(2)}, u32[]{:S(2)}) collective-permute-start(f32[128,48]{0,1:T(8,128)S(1)} %pad_maximum_fusion.13), channel_id=1, source_target_pairs={{0,3},{1,2},{2,1},{3,0},{4,7},{5,6},{6,5},{7,4},{8,11},{9,10},{10,... | collective-permute-start | bytes 73736 | tf_op jit(solution)/shard_map/ppermute | solution.py:70
  249.5 16.7 %collective-permute-start.15 = (bf16[128,1536]{1,0:T(8,128)(2,1)}, bf16[128,1536]{1,0:T(8,128)(2,1)S(1)}, u32[]{:S(2)}, u32[]{:S(2)}) collective-permute-start(bf16[128,1536]{1,0:T(8,128)(2,1)} %get-tuple-element.36), channel_id=1, source_target_pairs={{0,1},{1,0},{2,3},{3,2},{4,5},{5,4},{6,7},{7,6},{8,9},{9,8},{10,11... | collective-permute-start | bytes 1179656 | tf_op jit(solution)/shard_map/ppermute | solution.py:70
  250.6 30.1 %collective-permute-start.16 = (bf16[128,1536]{1,0:T(8,128)(2,1)}, bf16[128,1536]{1,0:T(8,128)(2,1)}, u32[]{:S(2)}, u32[]{:S(2)}) collective-permute-start(bf16[128,1536]{1,0:T(8,128)(2,1)} %get-tuple-element.38), channel_id=1, source_target_pairs={{0,2},{1,3},{2,0},{3,1},{4,6},{5,7},{6,4},{7,5},{8,10},{9,11},{10,... | collective-permute-start | bytes 1179656 | tf_op jit(solution)/shard_map/ppermute | solution.py:70
  252.5 28.2 %collective-permute-start.17 = (bf16[128,1536]{1,0:T(8,128)(2,1)}, bf16[128,1536]{1,0:T(8,128)(2,1)}, u32[]{:S(2)}, u32[]{:S(2)}) collective-permute-start(bf16[128,1536]{1,0:T(8,128)(2,1)} %get-tuple-element.37), channel_id=1, source_target_pairs={{0,3},{1,2},{2,1},{3,0},{4,7},{5,6},{6,5},{7,4},{8,11},{9,10},{10,... | collective-permute-start | bytes 1179656 | tf_op jit(solution)/shard_map/ppermute | solution.py:70
  254.7 30.9 %slice-start.2 = ((s8[4718592]{0:T(1024)(128)(4,1)}), s8[524288]{0:T(1024)(128)(4,1)S(1)}, s32[]{:S(2)}) async-start(s8[4718592]{0:T(1024)(128)(4,1)} %bitcast.365), calls=%async_computation.10 | async-start | bytes 1048576
  259.1 24.7 %copy-start.41 = (bf16[128,16]{0,1:T(8,128)(2,1)S(1)}, bf16[128,16]{0,1:T(8,128)(2,1)}, u32[]{:S(2)}) copy-start(bf16[128,16]{0,1:T(8,128)(2,1)} %copy-done.40) | copy-start | bytes 12292
  259.1 26.5 %slice-start.3 = ((s8[4718592]{0:T(1024)(128)(4,1)}), s8[4194304]{0:T(1024)(128)(4,1)S(1)}, s32[]{:S(2)}) async-start(s8[4718592]{0:T(1024)(128)(4,1)} %bitcast.365), calls=%async_computation.11 | async-start | bytes 8388608
  301.0 19.8 %all-to-all-start = ((bf16[8,128,512]{1,2,0:T(8,128)(2,1)}), bf16[8,128,512]{1,2,0:T(8,128)(2,1)}, u32[]{:S(2)}, u32[]{:S(2)}) async-start(bf16[8,128,512]{1,2,0:T(8,128)(2,1)} %pad_maximum_fusion.2), calls=%async_computation | async-start | bytes 2097152 | tf_op jit(solution)/shard_map/all_to_all | solution.py:246
  311.0 18.2 %copy-start.33 = (bf16[24576]{0:T(1024)(128)(2,1)S(1)}, bf16[24576]{0:T(1024)(128)(2,1)}, u32[]{:S(2)}) copy-start(bf16[24576]{0:T(1024)(128)(2,1)} %reshape.608) | copy-start | bytes 147460
  330.0 12.5 %all-to-all-start.1 = ((bf16[8,224,128]{2,1,0:T(8,128)(2,1)}), bf16[8,224,128]{2,1,0:T(8,128)(2,1)S(1)}, u32[]{:S(2)}, u32[]{:S(2)}) async-start(bf16[8,224,128]{2,1,0:T(8,128)(2,1)} %bitcast.418), calls=%async_computation.1 | async-start | bytes 917504 | tf_op jit(solution)/shard_map/all_to_all | solution.py:269
  333.5 107.5 %all-gather.20.cloned.1.call-start = ((), (), s32[]{:S(2)}) async-start(), calls=%async_computation.6 | async-start | bytes 2064384 | tf_op jit(solution)/shard_map/all_gather | solution.py:274
  336.3 25.6 %copy-start.13 = (bf16[286720]{0:T(1024)(128)(2,1)S(1)}, bf16[286720]{0:T(1024)(128)(2,1)}, u32[]{:S(2)}) copy-start(bf16[286720]{0:T(1024)(128)(2,1)} %reshape.614) | copy-start | bytes 1720324
  363.8 46.0 %all-to-all-start.2 = ((bf16[8,424,128]{2,1,0:T(8,128)(2,1)}), bf16[8,424,128]{2,1,0:T(8,128)(2,1)S(1)}, u32[]{:S(2)}, u32[]{:S(2)}) async-start(bf16[8,424,128]{2,1,0:T(8,128)(2,1)} %bitcast.388), calls=%async_computation.2 | async-start | bytes 1736704 | tf_op jit(solution)/shard_map/all_to_all | solution.py:269
  367.4 101.8 %all-gather.22.cloned.1.call-start = ((), (), s32[]{:S(2)}) async-start(), calls=%async_computation.7 | async-start | bytes 3907584 | tf_op jit(solution)/shard_map/all_gather | solution.py:274
  376.2 56.1 %copy-start.25 = (bf16[128,256]{1,0:T(8,128)(2,1)S(1)}, bf16[128,256]{1,0:T(8,128)(2,1)}, u32[]{:S(2)}) copy-start(bf16[128,256]{1,0:T(8,128)(2,1)} %copy-done.24) | copy-start | bytes 196612
  377.2 19.5 %collective-permute-start.6 = (bf16[128,1536]{1,0:T(8,128)(2,1)}, bf16[128,1536]{1,0:T(8,128)(2,1)}, u32[]{:S(2)}, u32[]{:S(2)}) collective-permute-start(bf16[128,1536]{1,0:T(8,128)(2,1)} %get-tuple-element.39), channel_id=1, source_target_pairs={{0,1},{1,0},{2,3},{3,2},{4,5},{5,4},{6,7},{7,6},{8,9},{9,8},{10,11... | collective-permute-start | bytes 1179656 | tf_op jit(solution)/shard_map/ppermute | solution.py:70
  377.2 30.0 %collective-permute-start.7 = (bf16[128,1536]{1,0:T(8,128)(2,1)}, bf16[128,1536]{1,0:T(8,128)(2,1)}, u32[]{:S(2)}, u32[]{:S(2)}) collective-permute-start(bf16[128,1536]{1,0:T(8,128)(2,1)} %get-tuple-element.41), channel_id=1, source_target_pairs={{0,2},{1,3},{2,0},{3,1},{4,6},{5,7},{6,4},{7,5},{8,10},{9,11},{10,... | collective-permute-start | bytes 1179656 | tf_op jit(solution)/shard_map/ppermute | solution.py:70
  379.2 28.1 %collective-permute-start.8 = (bf16[128,1536]{1,0:T(8,128)(2,1)}, bf16[128,1536]{1,0:T(8,128)(2,1)}, u32[]{:S(2)}, u32[]{:S(2)}) collective-permute-start(bf16[128,1536]{1,0:T(8,128)(2,1)} %get-tuple-element.40), channel_id=1, source_target_pairs={{0,3},{1,2},{2,1},{3,0},{4,7},{5,6},{6,5},{7,4},{8,11},{9,10},{10,... | collective-permute-start | bytes 1179656 | tf_op jit(solution)/shard_map/ppermute | solution.py:70
  (51 other events, 290.8 us)
Sparse Core Ops, SparseCore 0:
  30.5 45.1 all-gather.15
  77.6 38.8 all-gather.17
  119.0 23.4 all-gather.13
  362.0 30.0 all-gather.19
  432.4 33.5 all-gather.21

commit v2 on v1

v2 whole, which is shorter than its diff:
```python
import functools
import math

import jax
import jax.numpy as jnp
from jax import lax
from jax.experimental import pallas as pl
from jax.experimental.pallas import tpu as pltpu
from jax.sharding import PartitionSpec as P

HD = 128
EPS = 1e-06
ROPE_BASE = 1000000.0
ADAPTER_SCALE = 2.0
MASKED = -1e30
F32 = jnp.float32
BF16 = jnp.bfloat16


def dot_nn(a, b):
    return lax.dot_general(a, b, (((1,), (0,)), ((), ())), preferred_element_type=F32)


def dot_tn(a, b):
    return lax.dot_general(a, b, (((0,), (0,)), ((), ())), preferred_element_type=F32)


def dot_nt(a, b):
    return lax.dot_general(a, b, (((1,), (1,)), ((), ())), preferred_element_type=F32)


def inverse_norm(rows):
    return lax.rsqrt(jnp.mean(rows * rows, axis=-1, keepdims=True) + EPS)


def norm_pull(rows, inv, gain, grad):
    scaled = gain * grad
    return inv * scaled - rows * (inv * inv * inv) * jnp.mean(rows * scaled, axis=-1, keepdims=True)


def rope_tables(pos):
    half = HD // 2
    freq = ROPE_BASE ** (-jnp.arange(half, dtype=F32) * 2.0 / HD)
    angle = pos.astype(F32)[:, None] * freq[None, :]
    cosine, sine = jnp.cos(angle), jnp.sin(angle)
    return jnp.concatenate([cosine, cosine], axis=1), jnp.concatenate([-sine, sine], axis=1)


def row_positions(deal, rows, block):
    owner = rows // (2 * block)
    local = rows % (2 * block)
    table = jnp.arange(deal.shape[0], dtype=jnp.int32)
    pair = jnp.sum(jnp.where(owner[:, None] == table[None, :], deal[None, :], 0), axis=1)
    return jnp.where(
        local < block, pair * block + local, (2 * deal.shape[0] - 1 - pair) * block + local - block
    )


def ff_results_kernel(wa_ref, got_ref, bgu_ref, ad_ref, *, part_ff):
    n_ctx, n_wa, _, lanes = got_ref.shape
    own = wa_ref[0]
    rank = bgu_ref.shape[2]
    b_rows = bgu_ref.shape[0] * 2 * rank // n_ctx
    a_rows = ad_ref.shape[0] * rank // n_ctx
    starts = [j * part_ff // 128 * 128 for j in range(n_wa)]

    def write(read, store):
        left = None
        for j in range(n_wa):
            block = read(j).astype(F32)
            stop = starts[j + 1] - starts[j] if j + 1 < n_wa else lanes
            if left is not None:
                store(starts[j], block[:, :128] + left)
            first = 0 if left is None else 128
            store(starts[j] + first, block[:, first:stop])
            left = block[:, stop:] if stop < lanes else None

    for c in range(n_ctx):
        at = c * b_rows
        slot, half, low = at // (2 * rank), at // rank % 2, at % rank

        def put_b(lane, value):
            bgu_ref[slot, half, low : low + b_rows, lane : lane + value.shape[1]] = value

        write(lambda j: got_ref[c, own ^ j, :b_rows], put_b)
        at = c * a_rows
        slot, low = at // rank, at % rank

        def put_a(lane, value):
            ad_ref[slot, low : low + a_rows, lane : lane + value.shape[1]] = value

        write(lambda j: got_ref[c, own ^ j, b_rows:], put_a)


def ff_results(wa, got, slots, rank, part_ff):
    n_wa = got.shape[1]
    return pl.pallas_call(
        lambda *refs: ff_results_kernel(*refs, part_ff=part_ff),
        out_shape=(
            jax.ShapeDtypeStruct((slots, 2, rank, n_wa * part_ff), F32),
            jax.ShapeDtypeStruct((slots, rank, n_wa * part_ff), F32),
        ),
        in_specs=[pl.BlockSpec(memory_space=pltpu.SMEM), pl.BlockSpec(memory_space=pltpu.VMEM)],
        out_specs=(pl.BlockSpec(memory_space=pltpu.VMEM),) * 2,
        compiler_params=pltpu.CompilerParams(vmem_limit_bytes=48 << 20),
    )(wa, got)


def seq_results_kernel(wa_ref, index_ref, got_ref, *refs, layout):
    n_ctx, n_wa, share, third = got_ref.shape
    share = share // 3
    whole_refs, out_refs = refs[:n_wa], refs[n_wa:]
    own = wa_ref[0]
    slots = out_refs[0].shape[0]
    hot = [[index_ref[k] == slot for k in range(n_wa)] for slot in range(slots)]
    for c in range(n_ctx):
        for part in range(3):
            terms = [
                got_ref[c, own ^ j, part * share : (part + 1) * share, :].astype(F32)
                for j in range(n_wa)
            ]
            for slot in range(slots):
                total = jnp.zeros((share, third), F32)
                for j in range(n_wa):
                    total = total + jnp.where(index_ref[own ^ j] == slot, terms[j], 0.0)
                for out, first, count in layout:
                    low, high = max(first, c * share), min(first + count, (c + 1) * share)
                    if low >= high:
                        continue
                    value = total[low - c * share : high - c * share]
                    ref = out_refs[out]
                    if len(ref.shape) == 3:
                        lane = slice(part * third, (part + 1) * third)
                        ref[slot, low - first : high - first, lane] = value
                    elif part == 0:
                        wide = ref.shape[3]
                        for i in range(ref.shape[1]):
                            cut = value[:, i * wide : (i + 1) * wide]
                            ref[slot, i, low - first : high - first, :] = cut
    for slot in range(slots):
        total = jnp.zeros(whole_refs[0].shape, F32)
        for j in range(n_wa):
            value = jnp.zeros(whole_refs[0].shape, F32)
            for k in range(n_wa):
                take = jnp.logical_and(own ^ j == k, hot[slot][k])
                value = value + jnp.where(take, whole_refs[k][...].astype(F32), 0.0)
            total = total + value
        out_refs[0][slot] = total


def seq_results(wa, index_all, got, wholes, shapes, layout):
    smem = pl.BlockSpec(memory_space=pltpu.SMEM)
    vmem = pl.BlockSpec(memory_space=pltpu.VMEM)
    return pl.pallas_call(
        lambda *refs: seq_results_kernel(*refs, layout=layout),
        out_shape=tuple(jax.ShapeDtypeStruct(shape, F32) for shape in shapes),
        in_specs=[smem, smem] + [vmem] * (1 + len(wholes)),
        out_specs=(vmem,) * len(shapes),
        compiler_params=pltpu.CompilerParams(vmem_limit_bytes=48 << 20),
    )(wa, index_all, got, *wholes)


def local_call(kernel, out_shapes, *args, scratch=(), limit=56):
    vmem = pl.BlockSpec(memory_space=pltpu.VMEM)
    return pl.pallas_call(
        kernel,
        out_shape=tuple(jax.ShapeDtypeStruct(shape, kind) for shape, kind in out_shapes),
        in_specs=[vmem] * len(args),
        out_specs=(vmem,) * len(out_shapes),
        scratch_shapes=list(scratch),
        compiler_params=pltpu.CompilerParams(vmem_limit_bytes=limit << 20),
    )(*args)


def project_kernel(h1_ref, w_ref, a_ref, b_ref, bias_ref, sent_ref, u1_ref, *, q_cols):
    n_ctx, rows, wide = sent_ref.shape
    kv_cols = w_ref.shape[1] - q_cols
    h1 = h1_ref[...]
    u1 = dot_nt(h1, a_ref[...]).astype(BF16)
    u1_ref[...] = u1
    lin = dot_nn(h1, w_ref[...]) + bias_ref[...] + ADAPTER_SCALE * dot_nn(u1, b_ref[...])
    lin = lin.astype(BF16)
    pieces = [lin[c * rows : (c + 1) * rows, q_cols:] for c in range(n_ctx)]
    kv = jnp.concatenate(pieces, axis=1)
    fill = jnp.zeros((rows, wide - n_ctx * kv_cols - q_cols), BF16)
    for c in range(n_ctx):
        sent_ref[c, :, : n_ctx * kv_cols] = kv
        own = lin[c * rows : (c + 1) * rows, :q_cols]
        sent_ref[c, :, n_ctx * kv_cols :] = jnp.concatenate([own, fill], axis=1)


def turn(value, cosine, sine):
    return value * cosine + pltpu.roll(value, HD // 2, 1) * sine


def turn_back(value, cosine, sine):
    return value * cosine + pltpu.roll(value * sine, HD // 2, 1)


def heads_stacked(table, first, group):
    return jnp.concatenate(
        [table[:, (first + j) * HD : (first + j + 1) * HD] for j in range(group)], axis=0
    )


def attend_kernel(
    got_ref, cos_ref, sin_ref, kcos_ref, ksin_ref, qpos_ref, kpos_ref, x_ref, wo_ref, ao_ref,
    lo_ref, gain_ref, qb_ref, kb_ref, vb_ref, lse_ref, attn_ref, ob_ref, uo_ref, x1_ref, h2_ref,
):
    n_ctx = got_ref.shape[0]
    rows, width = x_ref.shape
    kvd = kb_ref.shape[1]
    kvh, heads = kvd // HD, width // HD
    group = heads // kvh
    q_cols, kv_cols = width // n_ctx, 2 * kvd // n_ctx
    scale = 1.0 / math.sqrt(HD)
    cosine, sine = cos_ref[...], sin_ref[...]
    q_lin = jnp.concatenate(
        [got_ref[c, :, 2 * kvd : 2 * kvd + q_cols] for c in range(n_ctx)], axis=1
    )
    for h in range(heads):
        lane = slice(h * HD, (h + 1) * HD)
        qb_ref[:, lane] = turn(q_lin[:, lane].astype(F32), cosine, sine).astype(BF16)
    for g in range(n_ctx):
        at = slice(g * rows, (g + 1) * rows)
        cut = slice(g * kv_cols, (g + 1) * kv_cols)
        kv_lin = jnp.concatenate([got_ref[c, :, cut] for c in range(n_ctx)], axis=1)
        kcos, ksin = kcos_ref[at, :], ksin_ref[at, :]
        for h in range(kvh):
            lane = slice(h * HD, (h + 1) * HD)
            kb_ref[at, lane] = turn(kv_lin[:, lane].astype(F32), kcos, ksin).astype(BF16)
        vb_ref[at, :] = kv_lin[:, kvd:]
    qpos = jnp.concatenate([qpos_ref[...]] * group, axis=0)
    seen = kpos_ref[...] <= qpos
    for g in range(kvh):
        q = heads_stacked(qb_ref, g * group, group)
        s = dot_nt(q, kb_ref[:, g * HD : (g + 1) * HD]) * scale
        s = jnp.where(seen, s, MASKED)
        top = jnp.max(s, axis=1, keepdims=True)
        e = jnp.exp(s - top)
        total = jnp.sum(e, axis=1, keepdims=True)
        lse_ref[g] = top + jnp.log(total)
        pb = (e * (1.0 / total)).astype(BF16)
        o = dot_nn(pb, vb_ref[:, g * HD : (g + 1) * HD])
        for j in range(group):
            lane = slice((g * group + j) * HD, (g * group + j + 1) * HD)
            attn_ref[:, lane] = o[j * rows : (j + 1) * rows]
    ob = attn_ref[...].astype(BF16)
    ob_ref[...] = ob
    uo = dot_nt(ob, ao_ref[...]).astype(BF16)
    uo_ref[...] = uo
    x1 = x_ref[...].astype(F32) + dot_nn(ob, wo_ref[...])
    x1 = x1 + ADAPTER_SCALE * dot_nn(uo, lo_ref[...])
    x1_ref[...] = x1
    h2_ref[...] = (x1 * inverse_norm(x1) * gain_ref[...]).astype(BF16)


def attend_back_kernel(*refs, n_wa, n_ctx):
    parts, refs = refs[:n_wa], refs[n_wa:]
    (
        agu_ref, gain_ref, x1_ref, g_ref, h2_ref, wo_ref, lo_ref, ao_ref, attn_ref, ob_ref, uo_ref,
        qb_ref, kb_ref, vb_ref, lse_ref, qpos_ref, kpos_ref, cos_ref, sin_ref, kcos_ref, ksin_ref,
        u1_ref, u1all_ref, dx1_ref, dlq_ref, sent_ref, ud_ref, dob, dq_acc, grads,
    ) = refs
    rows, width = x1_ref.shape
    keys, kvd = kb_ref.shape
    kvh, heads = kvd // HD, width // HD
    group = heads // kvh
    rank = uo_ref.shape[1]
    scale = 1.0 / math.sqrt(HD)
    got = parts[0][...].astype(F32)
    for part in parts[1:]:
        got = got + part[...].astype(F32)
    small = got[:, width : width + 3 * rank].astype(BF16)
    dug, ud = small[:, : 2 * rank], small[:, 2 * rank :]
    ud_ref[...] = ud
    d_h2 = got[:, :width] + dot_nn(dug, agu_ref[...])
    x1 = x1_ref[...]
    g = g_ref[...]
    d_x1 = g.astype(F32) + norm_pull(x1, inverse_norm(x1), gain_ref[...], d_h2)
    dx1_ref[...] = d_x1
    go = d_x1.astype(BF16)
    duo = (ADAPTER_SCALE * dot_nt(go, lo_ref[...])).astype(BF16)
    grads[: 2 * rank] = dot_tn(dug, h2_ref[...])
    grads[2 * rank : 3 * rank] = ADAPTER_SCALE * dot_tn(ud, g)
    grads[3 * rank : 4 * rank] = dot_tn(duo, ob_ref[...])
    grads[4 * rank : 5 * rank] = ADAPTER_SCALE * dot_tn(uo_ref[...], go)
    dob[...] = (dot_nt(go, wo_ref[...]) + dot_nn(duo, ao_ref[...])).astype(BF16)
    qpos = jnp.concatenate([qpos_ref[...]] * group, axis=0)
    step = math.gcd(keys, 1024)
    share = step // rows
    grads[6 * rank :] = jnp.zeros((2 * rank, width), F32)
    for kv in range(kvh):
        lane = slice(kv * HD, (kv + 1) * HD)
        v_lane = slice(kvd + kv * HD, kvd + (kv + 1) * HD)
        q = heads_stacked(qb_ref, kv * group, group)
        do = heads_stacked(dob, kv * group, group)
        o = heads_stacked(attn_ref, kv * group, group)
        delta = jnp.sum(do.astype(F32) * o, axis=1, keepdims=True)
        lse = lse_ref[kv]
        dq_acc[...] = jnp.zeros_like(dq_acc)

        def visit(turn_index):
            at = pl.ds(pl.multiple_of(turn_index * step, step), step)
            k = kb_ref[at, lane]
            s = dot_nt(q, k) * scale
            seen = kpos_ref[:, at] <= qpos
            p = jnp.exp(jnp.where(seen, s, MASKED) - lse)
            dp = dot_nt(do, vb_ref[at, lane])
            ds = (p * (dp - delta)).astype(BF16)
            dq_acc[...] += dot_nn(ds, k)
            dk = turn_back(dot_tn(ds, q) * scale, kcos_ref[at, :], ksin_ref[at, :]).astype(BF16)
            dv = dot_tn(p.astype(BF16), do).astype(BF16)
            u1 = u1all_ref[at, :]
            grads[6 * rank : 7 * rank, lane] += dot_tn(u1[:, rank : 2 * rank], dk)
            grads[6 * rank : 7 * rank, v_lane] += dot_tn(u1[:, 2 * rank :], dv)
            owners = pl.ds(turn_index * share, share)
            sent_ref[owners, :rows, lane] = dk.reshape(share, rows, HD)
            sent_ref[owners, :rows, v_lane] = dv.reshape(share, rows, HD)

        if keys == step:
            visit(0)
        else:
            pl.loop(0, keys // step)(visit)
        for j in range(group):
            head = slice((kv * group + j) * HD, (kv * group + j + 1) * HD)
            dq = dq_acc[j * rows : (j + 1) * rows] * scale
            dlq_ref[:, head] = turn_back(dq, cos_ref[...], sin_ref[...]).astype(BF16)
    grads[5 * rank : 6 * rank] = ADAPTER_SCALE * dot_tn(u1_ref[:, :rank], dlq_ref[...])
    grads[6 * rank : 7 * rank] = grads[6 * rank : 7 * rank] * ADAPTER_SCALE
    count = 8 * rank // n_ctx
    third = width // 3
    for c in range(n_ctx):
        for i in range(3):
            at = rows + i * count
            value = grads[c * count : (c + 1) * count, i * third : (i + 1) * third]
            sent_ref[c, at : at + count, :] = value.astype(BF16)


def collect_kernel(got_ref, dlq_ref, bq_ref, bkv_ref, dlkv_ref, du1_ref, share_ref):
    rows = dlq_ref.shape[0]
    rank = bq_ref.shape[0]
    kvd = bkv_ref.shape[2]
    total = got_ref[0].astype(F32)
    for c in range(1, got_ref.shape[0]):
        total = total + got_ref[c].astype(F32)
    dlkv = total[:rows].astype(BF16)
    dlkv_ref[...] = dlkv
    share_ref[...] = total[rows:].astype(BF16)
    du1 = [
        dot_nt(dlq_ref[...], bq_ref[...]),
        dot_nt(dlkv[:, :kvd], bkv_ref[0]),
        dot_nt(dlkv[:, kvd:], bkv_ref[1]),
    ]
    du1_ref[...] = (ADAPTER_SCALE * jnp.concatenate(du1, axis=1)).astype(BF16)


def finish_kernel(*refs, n_wa):
    parts, refs = refs[:n_wa], refs[n_wa:]
    (
        x1_ref, ud_ref, ld_ref, x_ref, gain_ref, dx1_ref, dlq_ref, dlkv_ref, du1_ref, w_ref, a_ref,
        out_ref, gx_ref,
    ) = refs
    n_ctx = w_ref.shape[0]
    q_cols, kv_cols = dlq_ref.shape[1] // n_ctx, dlkv_ref.shape[1] // n_ctx
    out = x1_ref[...] + ADAPTER_SCALE * dot_nn(ud_ref[...], ld_ref[...])
    for part in parts:
        out = out + part[...].astype(F32)
    out_ref[...] = out.astype(BF16)
    d_h1 = dot_nn(du1_ref[...], a_ref[...])
    for c in range(n_ctx):
        block = jnp.concatenate(
            [
                dlq_ref[:, c * q_cols : (c + 1) * q_cols],
                dlkv_ref[:, c * kv_cols : (c + 1) * kv_cols],
            ],
            axis=1,
        )
        d_h1 = d_h1 + dot_nt(block, w_ref[c])
    x = x_ref[...].astype(F32)
    gx_ref[...] = dx1_ref[...] + norm_pull(x, inverse_norm(x), gain_ref[...], d_h1)


def mlp_kernel(*refs, chunks, part_ff, tile, last):
    refs = list(refs)
    index_ref, shift_ref = refs[:2]
    h2_refs, g_refs = refs[2 : 2 + chunks], refs[2 + chunks : 2 + 2 * chunks]
    refs = refs[2 + 2 * chunks :]
    agu_ref, ld_ref, gu_ref, down_ref, lift_ref, ad_ref, prior_ref = refs[:7]
    refs = refs[7:]
    out_refs, dh_refs = refs[:chunks], refs[chunks : 2 * chunks]
    grads_ref = refs[2 * chunks]
    h2, gd, low, low_t, out_acc, dh_acc, small_acc, grads = refs[2 * chunks + 1 :]
    rows, width = h2_refs[0].shape
    slots, _, rank, _ = lift_ref.shape
    span = slots * rank
    step, steps = pl.program_id(0), pl.num_programs(0)

    def row_slot(lanes):
        return jnp.concatenate(
            [jnp.full((rows, lanes), index_ref[k], jnp.int32) for k in range(chunks)], axis=0
        )

    @pl.when(step == 0)
    def _():
        for k in range(chunks):
            h2[k * rows : (k + 1) * rows, :] = h2_refs[k][...]
            gd[k * rows : (k + 1) * rows, :] = g_refs[k][...]
        out_acc[...] = jnp.zeros_like(out_acc)
        dh_acc[...] = jnp.zeros_like(dh_acc)
        small_acc[...] = jnp.zeros_like(small_acc)
        grads[...] = prior_ref[...]
        lane = lax.broadcasted_iota(jnp.int32, (chunks * rows, span), 1)
        own = lane // rank == row_slot(span)
        flat_a = agu_ref[...]
        parts = [
            dot_nt(h2[...], flat_a[:, :rank].reshape(span, width)).astype(BF16),
            dot_nt(h2[...], flat_a[:, rank:].reshape(span, width)).astype(BF16),
            dot_nt(gd[...], ld_ref[...].reshape(span, width)).astype(BF16),
        ]
        for i, part in enumerate(parts):
            value = jnp.where(own, part.astype(F32) * ADAPTER_SCALE, 0.0)
            low[i] = value.astype(BF16)
            low_t[i] = value.T.astype(BF16)

    def work(first, wide):
        lanes = pl.ds(first, wide)
        w_g, w_u = gu_ref[0, :wide, :], gu_ref[1, :wide, :]
        w_d = down_ref[:wide, :]
        l_g = lift_ref[:, 0, :, :wide].reshape(span, wide)
        l_u = lift_ref[:, 1, :, :wide].reshape(span, wide)
        a_d = ad_ref[:, :, :wide].reshape(span, wide)
        gate = dot_nt(h2[...], w_g) + dot_nn(low[0], l_g)
        up = dot_nt(h2[...], w_u) + dot_nn(low[1], l_u)
        sigma = 1.0 / (1.0 + jnp.exp(-gate))
        swish = gate * sigma
        hidden = (swish * up).astype(BF16)
        d_hidden = dot_nt(gd[...], w_d) + dot_nn(low[2], a_d)
        d_gate = (d_hidden * up * (sigma + swish * (1.0 - sigma))).astype(BF16)
        d_up = (d_hidden * swish).astype(BF16)
        out_acc[...] += dot_nn(hidden, w_d)
        dh_acc[...] += dot_nn(d_gate, w_g) + dot_nn(d_up, w_u)
        small_acc[0] += dot_nt(d_gate, l_g)
        small_acc[1] += dot_nt(d_up, l_u)
        small_acc[2] += dot_nt(hidden, a_d)
        grads[0, :, lanes] += dot_nn(low_t[0], d_gate)
        grads[1, :, lanes] += dot_nn(low_t[1], d_up)
        grads[2, :, lanes] += dot_nn(low_t[2], hidden)

    rest = part_ff % tile
    if rest:
        pl.when(step < steps - 1)(lambda: work(pl.multiple_of(step * tile, tile), tile))
        pl.when(step == steps - 1)(lambda: work(part_ff - rest, rest))
    else:
        work(pl.multiple_of(step * tile, tile), tile)

    @pl.when(step == steps - 1)
    def _():
        for k in range(chunks):
            at = slice(k * rows, (k + 1) * rows)
            out_refs[k][...] = out_acc[at, :].astype(BF16)
            dh_refs[k][:, :width] = dh_acc[at, :].astype(BF16)
            picked = []
            for i in range(3):
                value = jnp.zeros((rows, rank), F32)
                for slot in range(slots):
                    mine = small_acc[i, at, slot * rank : (slot + 1) * rank]
                    value = value + jnp.where(index_ref[k] == slot, mine, 0.0)
                picked.append(value * (ADAPTER_SCALE if i < 2 else 1.0))
            picked.append(jnp.zeros((rows, 128 - 3 * rank), F32))
            dh_refs[k][:, width:] = jnp.concatenate(picked, axis=1).astype(BF16)
        if not last:
            grads_ref[...] = grads[...]
        else:
            n_ctx = grads_ref.shape[0]
            b_rows, a_rows = 2 * span // n_ctx, span // n_ctx
            odd = shift_ref[0] != 0
            tables = []
            for i in range(3):
                value = grads[i]
                if rest % 128:
                    value = jnp.where(odd, pltpu.roll(value, part_ff % 128, 1), value)
                tables.append(value.astype(BF16))
            for c in range(n_ctx):
                at = c * b_rows
                slot, half, at = at // (2 * rank), at // rank % 2, at % rank
                at += slot * rank
                grads_ref[c, :b_rows, :] = tables[half][at : at + b_rows]
                grads_ref[c, b_rows:, :] = tables[2][c * a_rows : (c + 1) * a_rows]


def mlp_call(index, shift, h2s, gs, a_gu, lift_down, w_gu, w_down, lift, a_down, prior, n_ctx):
    chunks = len(h2s)
    rows, width = h2s[0].shape
    part_ff = w_down.shape[0]
    slots, _, rank, _ = lift.shape
    span = slots * rank
    tile = 256
    steps = -(-part_ff // tile)
    lanes = prior.shape[2]
    smem = pl.BlockSpec(memory_space=pltpu.SMEM)

    def whole(shape):
        return pl.BlockSpec(shape, lambda i: (0,) * len(shape))

    if n_ctx is None:
        grads_shape = jax.ShapeDtypeStruct((3, span, lanes), F32)
    else:
        grads_shape = jax.ShapeDtypeStruct((n_ctx, 3 * span // n_ctx, lanes), BF16)
    total = chunks * rows
    outs = pl.pallas_call(
        lambda *refs: mlp_kernel(
            *refs, chunks=chunks, part_ff=part_ff, tile=tile, last=n_ctx is not None
        ),
        grid=(steps,),
        out_shape=(jax.ShapeDtypeStruct((rows, width), BF16),) * chunks
        + (jax.ShapeDtypeStruct((rows, width + 128), BF16),) * chunks
        + (grads_shape,),
        in_specs=[smem, smem]
        + [whole((rows, width))] * (2 * chunks)
        + [
            whole(a_gu.shape),
            whole(lift_down.shape),
            pl.BlockSpec((2, tile, width), lambda i: (0, i, 0)),
            pl.BlockSpec((tile, width), lambda i: (i, 0)),
            pl.BlockSpec((slots, 2, rank, tile), lambda i: (0, 0, 0, i)),
            pl.BlockSpec((slots, rank, tile), lambda i: (0, 0, i)),
            whole(prior.shape),
        ],
        out_specs=(whole((rows, width)),) * chunks
        + (whole((rows, width + 128)),) * chunks
        + (whole(grads_shape.shape),),
        scratch_shapes=[
            pltpu.VMEM((total, width), BF16),
            pltpu.VMEM((total, width), BF16),
            pltpu.VMEM((3, total, span), BF16),
            pltpu.VMEM((3, span, total), BF16),
            pltpu.VMEM((total, width), F32),
            pltpu.VMEM((total, width), F32),
            pltpu.VMEM((3, total, span), F32),
            pltpu.VMEM((3, span, lanes), F32),
        ],
        compiler_params=pltpu.CompilerParams(vmem_limit_bytes=50 << 20),
        cost_estimate=pl.CostEstimate(
            flops=12 * total * width * part_ff,
            bytes_accessed=6 * width * part_ff,
            transcendentals=0,
        ),
    )(index, shift, *h2s, *gs, a_gu, lift_down, w_gu, w_down, lift, a_down, prior)
    return outs[:chunks], outs[chunks : 2 * chunks], outs[-1]


def swap(value, axis, count, k):
    return lax.ppermute(value, axis, [(i, i ^ k) for i in range(count)])


def make_per_device(n_ctx, n_wa):
    def wa_exchange(value):
        return [value] + [swap(value, "wa", n_wa, k) for k in range(1, n_wa)]

    def absolute(parts, axis):
        stacked = jnp.stack(parts)
        own = lax.axis_index(axis)
        return jnp.take(stacked, jnp.arange(len(parts)) ^ own, axis=0)

    def rows_over_wa(shard):
        part = shard.shape[0] // n_ctx
        mine = lax.dynamic_slice_in_dim(shard, lax.axis_index("ctx") * part, part, 0)
        return absolute(wa_exchange(mine), "wa")

    def rows_over_ctx(over_wa):
        got = lax.all_gather(over_wa, "ctx", axis=0, tiled=False)
        return got.transpose(1, 0, 2, 3).reshape(-1, over_wa.shape[2])

    def per_device(
        tokens,
        cotangent,
        adapter_index,
        deal,
        w_qkv,
        b_qkv,
        w_o,
        w_gu,
        w_down,
        gain_attn,
        gain_mlp,
        a_qkv,
        b_q,
        b_kv,
        a_o,
        lift_o,
        a_gu,
        lift_gu,
        a_down,
        lift_down,
    ):
        rows, width = tokens.shape[1:]
        block = rows // 2
        rank = b_q.shape[1]
        slots = a_qkv.shape[0]
        kvd = b_kv.shape[3]
        heads = width // HD
        kvh = kvd // HD
        group = heads // kvh
        part_ff = w_down.shape[0]
        wa = lax.axis_index("wa")
        ctx = lax.axis_index("ctx")
        chosen = adapter_index[0]

        def picked(table):
            return lax.dynamic_index_in_dim(table, chosen, 0, keepdims=False)

        grad_out_bf = cotangent[0]
        x_bf = tokens[0]
        q_cols, kv_cols = width // n_ctx, 2 * kvd // n_ctx
        gain_one = gain_attn.astype(F32)[None]
        gain_two = gain_mlp.astype(F32)[None]
        s_aqkv, s_bq, s_bkv = picked(a_qkv), picked(b_q), picked(b_kv)
        s_ao, s_lo, s_agu, s_ld = picked(a_o), picked(lift_o), picked(a_gu), picked(lift_down)

        x = x_bf.astype(F32)
        h1 = (x * inverse_norm(x) * gain_one).astype(BF16)
        h1_all = lax.all_gather(h1, "ctx", axis=0, tiled=True)

        def block_of(table):
            return jnp.concatenate(
                [
                    lax.dynamic_slice_in_dim(table[:, :width], ctx * q_cols, q_cols, 1),
                    lax.dynamic_slice_in_dim(table[:, width:], ctx * kv_cols, kv_cols, 1),
                ],
                axis=1,
            )

        w_block = absolute(wa_exchange(block_of(w_qkv)), "wa").reshape(width, q_cols + kv_cols)
        w_block, w_o = lax.optimization_barrier((w_block, w_o))
        index_all = jnp.concatenate(wa_exchange(adapter_index))
        o_wa = rows_over_wa(w_o)
        o_wa, grad_sent = lax.optimization_barrier((o_wa, grad_out_bf))
        b_all = jnp.concatenate(
            [
                jnp.pad(s_bq, ((0, 0), (0, 2 * kvd))),
                jnp.pad(s_bkv[0], ((0, 0), (width, kvd))),
                jnp.pad(s_bkv[1], ((0, 0), (width + kvd, 0))),
            ],
            axis=0,
        )
        key_pos = row_positions(deal, jnp.arange(n_ctx * rows, dtype=jnp.int32), block)
        key_cos, key_sin = rope_tables(key_pos)

        def own_rows(table):
            return lax.dynamic_slice_in_dim(table, ctx * rows, rows, 0)

        query_pos, cosine, sine = own_rows(key_pos)[:, None], own_rows(key_cos), own_rows(key_sin)
        key_pos = key_pos[None]
        sent, u1_all = local_call(
            functools.partial(project_kernel, q_cols=q_cols),
            [
                ((n_ctx, rows, -(-(2 * kvd + q_cols) // 128) * 128), BF16),
                ((n_ctx * rows, 3 * rank), BF16),
            ],
            h1_all,
            w_block,
            s_aqkv,
            block_of(b_all),
            block_of(b_qkv[None]).astype(F32),
        )
        grads_all = wa_exchange(grad_sent)
        got = lax.all_to_all(sent, "ctx", 0, 0, tiled=True)
        u1 = own_rows(u1_all)
        full_o = rows_over_ctx(o_wa)
        w_blocks = lax.all_gather(w_block, "ctx", axis=0, tiled=False)
        qb, kb, vb, lse, attn, ob, uo, x1, h2 = local_call(
            attend_kernel,
            [
                ((rows, width), BF16),
                ((n_ctx * rows, kvd), BF16),
                ((n_ctx * rows, kvd), BF16),
                ((kvh, group * rows, 1), F32),
                ((rows, width), F32),
                ((rows, width), BF16),
                ((rows, rank), BF16),
                ((rows, width), F32),
                ((rows, width), BF16),
            ],
            got,
            cosine,
            sine,
            key_cos,
            key_sin,
            query_pos,
            key_pos,
            x_bf,
            full_o,
            s_ao,
            s_lo,
            gain_two,
        )
        h2, *grads_all = lax.optimization_barrier((h2, *grads_all))

        first = wa * part_ff
        lift_part = lax.dynamic_slice_in_dim(lift_gu, first, part_ff, 3)
        down_part = lax.dynamic_slice_in_dim(a_down, first, part_ff, 2)
        lanes = -(-max(part_ff + j * part_ff % 128 for j in range(n_wa)) // 128) * 128
        ff_grads = jnp.zeros((3, slots * rank, lanes), F32)
        shift = (first % 128).astype(jnp.int32)[None]
        w_gu_t = w_gu.transpose(0, 2, 1)
        h2_all = wa_exchange(h2)
        out_sent, d_h2_sent = {}, {}
        groups = [[1, 2], [3, 0]]
        for at, group_wa in enumerate(groups):
            done = mlp_call(
                jnp.concatenate([index_all[k : k + 1] for k in group_wa]),
                shift,
                [h2_all[k] for k in group_wa],
                [grads_all[k] for k in group_wa],
                a_gu,
                lift_down,
                w_gu_t,
                w_down,
                lift_part,
                down_part,
                ff_grads,
                n_ctx if at == len(groups) - 1 else None,
            )
            for k, part, d_part in zip(group_wa, done[0], done[1]):
                out_sent[k], d_h2_sent[k] = part, d_part
            ff_grads = done[2]

        def wa_return(parts):
            return [parts[0]] + [swap(parts[k], "wa", n_wa, k) for k in range(1, n_wa)]

        d_h2_parts = wa_return(d_h2_sent)
        ff_got = lax.all_to_all(ff_grads, "ctx", 0, 0, tiled=True)
        ff_share = jnp.sum(ff_got.astype(F32), axis=0).astype(BF16)
        ff_share, *d_h2_parts = lax.optimization_barrier((ff_share, *d_h2_parts))
        ff_wa = jnp.stack(wa_exchange(ff_share))
        count = 8 * rank // n_ctx
        d_x1, dl_q, sent, ud = local_call(
            functools.partial(attend_back_kernel, n_wa=n_wa, n_ctx=n_ctx),
            [
                ((rows, width), F32),
                ((rows, width), BF16),
                ((n_ctx, rows + 3 * count, 2 * kvd), BF16),
                ((rows, rank), BF16),
            ],
            *d_h2_parts,
            s_agu,
            gain_two,
            x1,
            grad_out_bf,
            h2,
            full_o,
            s_lo,
            s_ao,
            attn,
            ob,
            uo,
            qb,
            kb,
            vb,
            lse,
            query_pos,
            key_pos,
            cosine,
            sine,
            key_cos,
            key_sin,
            u1,
            u1_all,
            scratch=[
                pltpu.VMEM((rows, width), BF16),
                pltpu.VMEM((group * rows, HD), F32),
                pltpu.VMEM((8 * rank, width), F32),
            ],
        )
        sent, ff_wa = lax.optimization_barrier((sent, ff_wa))
        got = lax.all_to_all(sent, "ctx", 0, 0, tiled=True)
        out_parts = wa_return(out_sent)
        ff_all = lax.all_gather(ff_wa, "ctx", axis=0, tiled=False)
        dl_kv, du1, share = local_call(
            collect_kernel,
            [
                ((rows, 2 * kvd), BF16),
                ((rows, 3 * rank), BF16),
                ((3 * count, 2 * kvd), BF16),
            ],
            got,
            dl_q,
            s_bq,
            s_bkv,
        )
        du1_sent = jnp.broadcast_to(du1[None], (n_ctx,) + du1.shape)
        du1_all = lax.all_to_all(du1_sent, "ctx", 0, 0, tiled=True).reshape(-1, 3 * rank)
        seq_all = lax.all_gather(jnp.stack(wa_exchange(share)), "ctx", axis=0, tiled=False)
        g_aqkv = dot_tn(du1_all, h1_all).astype(BF16)
        g_aqkv_all = wa_exchange(g_aqkv)
        out, grad_x = local_call(
            functools.partial(finish_kernel, n_wa=n_wa),
            [((rows, width), BF16), ((rows, width), F32)],
            *out_parts,
            x1,
            ud,
            s_ld,
            x_bf,
            gain_one,
            d_x1,
            dl_q,
            dl_kv,
            du1,
            w_blocks,
            s_aqkv,
        )
        own_wa = wa.astype(jnp.int32)[None]
        r_bgu, r_ad = ff_results(own_wa, ff_all, slots, rank, part_ff)
        shapes = [
            a_qkv.shape,
            a_gu.shape,
            lift_down.shape,
            a_o.shape,
            lift_o.shape,
            b_q.shape,
            b_kv.shape,
        ]
        layout, at = [], 0
        for i, tall in enumerate([2 * rank, rank, rank, rank, rank, rank]):
            layout.append((i + 1, at, tall))
            at += tall
        r_aqkv, r_agu, r_ld, r_ao, r_lo, r_bq, r_bkv = seq_results(
            own_wa, index_all, seq_all, g_aqkv_all, shapes, layout
        )
        return (
            out[None],
            grad_x[None],
            r_aqkv,
            r_bq,
            r_bkv,
            r_ao,
            r_lo,
            r_agu,
            r_bgu,
            r_ad,
            r_ld,
        )

    return per_device


def solution(mesh):
    rep = P()
    return jax.shard_map(
        make_per_device(mesh.shape["ctx"], mesh.shape["wa"]),
        mesh=mesh,
        in_specs=(
            P("wa", "ctx", None),
            P("wa", "ctx", None),
            P("wa"),
            rep,
            P("wa", None),
            rep,
            P("wa", None),
            P(None, None, "wa"),
            P("wa", None),
        )
        + (rep,) * 11,
        out_specs=(P("wa", "ctx", None), P("wa", "ctx", None)) + (rep,) * 9,
        check_vma=False,
    )
```

time: 543 us -> 388 us (0.71)
  matrix products: 104 us -> 2.53 us
  Pallas kernels: 0 us -> 89.6 us
  blocking collectives: 80.4 us -> 0 us
  local copies, waits for them, and re-layouts: 115 us -> 38.7 us
  starting transfers between devices: 43.2 us -> 67 us
  other arithmetic: 43.2 us -> 22.2 us
  waiting for transfers between devices: 134 us -> 148 us
    pallas_call x0 -> x9, Pallas kernels: none -> 89.6 us  [the longest x2 43 us: mlp_call(): pl.pallas_call(lambda *refs: mlp_kernel(*refs, chunks=chunks, part_ff=par...]
    dot_general x38 -> x0, matrix products: 88.3 us -> none  [the longest x16 41.9 us: dot_nn(): lax.dot_general(a, b, (((1,), (0,)), ((), ())), preferred_element_type=F32)]
    all_gather x4 -> x0, blocking collectives: 80.4 us -> none  [the longest x2 41.7 us: share_all(): over_wa = lax.all_gather(share, 'wa', axis=0, tiled=False)]
    reshape x19 -> x0, local copies, waits for them, and re-layouts: 44.2 us -> none  [the longest x3 21.7 us: per_device(): r_bgu.transpose(1, 2, 3, 0, 4).reshape(slots, 2, rank, n_wa * part_ff)]
    all_gather x5, waiting for transfers between devices: 53.9 us -> 19.7 us  [the longest x1 19.7 us: rows_over_ctx(): got = lax.all_gather(over_wa, 'ctx', axis=0, tiled=False)]
    unnamed x166 -> x64, local copies, waits for them, and re-layouts: 44.3 us -> 10.3 us
    ppermute x18 -> x30, waiting for transfers between devices: 69.1 us -> 98.4 us  [swap(): return lax.ppermute(value, axis, [(i, i ^ k) for i in range(count)])]
    ppermute x18 -> x30, starting transfers between devices: 31.6 us -> 49.6 us  [swap(): return lax.ppermute(value, axis, [(i, i ^ k) for i in range(count)])]
  transfers between devices with their start and end apart: 26 -> 39, of which waited for: 11 -> 17; matrix products, arithmetic and copies ran while one was open for 23% -> 13% of each run, Pallas kernels for 0% -> 23%
where the time goes in v2:
time: 388 us; the launch traced here: 383 us
  waiting for transfers between devices  148 us (38%)
  Pallas kernels  89.6 us (23%)
  starting transfers between devices  67 us (17%)
  local copies, waits for them, and re-layouts  38.7 us (10%)
  other arithmetic  22.2 us (6%)
  between operations  15.2 us (4%)
    ppermute x30, waiting for transfers between devices, swap(): return lax.ppermute(value, axis, [(i, i ^ k) for i in range(count)])  98.4 us
    ppermute x30, starting transfers between devices, swap(): return lax.ppermute(value, axis, [(i, i ^ k) for i in range(count)])  49.6 us
    pallas_call x2, Pallas kernels, mlp_call(): pl.pallas_call(lambda *refs: mlp_kernel(*refs, chunks=chunks, part_ff=par...  43 us
    pallas_call x5, Pallas kernels, local_call(): pl.pallas_call(kernel, out_shape=tuple((jax.ShapeDtypeStruct(shape, kind)...  39.2 us
    all_gather x1, waiting for transfers between devices, rows_over_ctx(): got = lax.all_gather(over_wa, 'ctx', axis=0, tiled=False)  19.7 us
    all_to_all x2, waiting for transfers between devices, per_device(): got = lax.all_to_all(sent, 'ctx', 0, 0, tiled=True)  18.2 us
    unnamed x64, local copies, waits for them, and re-layouts  10.3 us
    all_to_all x2, starting transfers between devices, per_device(): got = lax.all_to_all(sent, 'ctx', 0, 0, tiled=True)  9.09 us
  transfers between devices with their start and end apart: 39, of which 17 were waited for; matrix products, arithmetic and copies ran while one was open for 13% of the time, Pallas kernels for 23%

profile of v2, /device:TPU:0, one launch (start us, length us, event | category | flops | bytes accessed | tf_op | source)
XLA Modules:
  0.0 382.9 jit_solution(7545624546518154336)
XLA Ops:
  11.2 2.4 slice.26
  14.9 3.1 collective-permute-start.1
  18.0 2.6 collective-permute-start.2
  20.9 5.5 %collective-permute-done.1 = bf16[384,256]{1,0:T(8,128)(2,1)S(1)} collective-permute-done((bf16[384,256]{1,0:T(8,128)(2,1)S(1)}, bf16[384,256]{1,0:T(8,128)(2,1)S(1)}, u32[]{:S(2)}, u32[]{:S(2)}) %collective-permute-start.1) | collective-permute-done | bytes 196640 | tf_op jit(solution)/shard_map/ppermute | solution.py:554
  26.4 8.8 %collective-permute-done.2 = bf16[384,256]{1,0:T(8,128)(2,1)S(1)} collective-permute-done((bf16[384,256]{1,0:T(8,128)(2,1)S(1)}, bf16[384,256]{1,0:T(8,128)(2,1)S(1)}, u32[]{:S(2)}, u32[]{:S(2)}) %collective-permute-start.2) | collective-permute-done | bytes 196640 | tf_op jit(solution)/shard_map/ppermute | solution.py:554
  38.4 2.3 bitcast_select_fusion.w_ref
  41.6 3.4 collective-permute-start.4
  49.7 8.3 %collective-permute-done.5 = bf16[48,1536]{1,0:T(8,128)(2,1)S(1)} collective-permute-done((bf16[48,1536]{1,0:T(8,128)(2,1)S(1)}, bf16[48,1536]{1,0:T(8,128)(2,1)S(1)}, u32[]{:S(2)}, u32[]{:S(2)}) %collective-permute-start.5) | collective-permute-done | bytes 147488 | tf_op jit(solution)/shard_map/ppermute | solution.py:554
  60.4 2.2 collective-permute-start.11
  69.3 5.3 %shard_map.275 = (bf16[8,128,768]{2,1,0:T(8,128)(2,1)}, bf16[1024,48]{1,0:T(8,128)(2,1)}) custom-call(bf16[1024,1536]{1,0:T(8,128)(2,1)} %all-gather.10.cloned.1.call-done.h1_ref, bf16[1536,256]{1,0:T(8,128)(2,1)} %bitcast_select_fusion.w_ref, bf16[48,1536]{1,0:T(8,128)(2,1)} %dynamic-slice_bitcast_fusion.a_ref.refs_14_, ...), custom_call_target="tpu_custom_call" | custom-call | tf_op jit(solution)/shard_map/pallas_call | solution.py:165
  74.6 4.8 %all-to-all-start = ((bf16[8,128,768]{2,1,0:T(8,128)(2,1)}), bf16[8,128,768]{2,1,0:T(8,128)(2,1)}, u32[]{:S(2)}, u32[]{:S(2)}) async-start(bf16[8,128,768]{2,1,0:T(8,128)(2,1)} %get-tuple-element.67), calls=%async_computation | async-start | bytes 3145728 | tf_op jit(solution)/shard_map/all_to_all | solution.py:668
  87.7 2.2 collective-permute-start.9
  92.3 19.7 %all-gather.12.cloned.1.call-done = bf16[32,48,1536]{2,1,0:T(8,128)(2,1)} async-done(((bf16[4,48,1536]{2,1,0:T(8,128)(2,1)}), bf16[32,48,1536]{2,1,0:T(8,128)(2,1)}) %all-gather.12.cloned.1.call-update) | async-done | bytes 4718608 | tf_op jit(solution)/shard_map/all_gather | solution.py:572
  112.0 4.9 %copy.43 = bf16[8,4,48,1536]{3,2,0,1:T(8,128)(2,1)} copy(bf16[8,4,48,1536]{3,2,1,0:T(8,128)(2,1)} %bitcast.84) | data formatting | bytes 9437184 | tf_op jit(solution)/shard_map/all_gather | solution.py:572
  116.9 10.3 %shard_map.276 = (bf16[128,1536]{1,0:T(8,128)(2,1)}, bf16[1024,256]{1,0:T(8,128)(2,1)}, bf16[1024,256]{1,0:T(8,128)(2,1)}, f32[2,768,1]{2,1,0:T(8,128)}, f32[128...) custom-call(bf16[8,128,768]{2,1,0:T(8,128)(2,1)} %all-to-all-done.go, ...), custom_call_target="tpu_custom_call" | custom-call | tf_op jit(solution)/shard_map/pallas_call | solution.py:165
  127.9 3.1 collective-permute-start
  135.7 3.1 collective-permute-start.10
  138.8 10.3 %collective-permute-done.13.refs_2_ = bf16[128,1536]{1,0:T(8,128)(2,1)S(1)} collective-permute-done((bf16[128,1536]{1,0:T(8,128)(2,1)}, bf16[128,1536]{1,0:T(8,128)(2,1)S(1)}, u32[]{:S(2)}, u32[]{:S(2)}) %collective-permute-start.13) | collective-permute-done | bytes 393248 | tf_op jit(solution)/shard_map/ppermute | solution.py:554
  149.9 11.3 %collective-permute-done.14.refs_3_ = bf16[128,1536]{1,0:T(8,128)(2,1)S(1)} collective-permute-done((bf16[128,1536]{1,0:T(8,128)(2,1)}, bf16[128,1536]{1,0:T(8,128)(2,1)S(1)}, u32[]{:S(2)}, u32[]{:S(2)}) %collective-permute-start.14) | collective-permute-done | bytes 393248 | tf_op jit(solution)/shard_map/ppermute | solution.py:554
  163.3 21.8 %shard_map.277 = (bf16[128,1536]{1,0:T(8,128)(2,1)S(1)}, bf16[128,1536]{1,0:T(8,128)(2,1)S(1)}, bf16[128,1664]{1,0:T(8,128)(2,1)S(1)}, bf16[128,1664]{1,0:T(8,128)(2,1)S(1)}, f32[3,64,2304]{2,1,0:T(8,128)}) custom-call(s32[2]{0:T(128)S(1)} %pad_add_fusion.1.refs_0_, s32[1]{0:T(128)} %bitcast.refs_1_, bf16[128,1536]{1,0:T(8,128)(2,1)S(1)} %copy-done.19, ...), custom_call_target="tpu_custom_call" | custom-call | flops 10569646080 | bytes 20643840 | tf_op jit(solution)/shard_map/pallas_call | solution.py:511
  185.8 21.2 %shard_map.278 = (bf16[128,1536]{1,0:T(8,128)(2,1)S(1)}, bf16[128,1536]{1,0:T(8,128)(2,1)S(1)}, bf16[128,1664]{1,0:T(8,128)(2,1)S(1)}, bf16[128,1664]{1,0:T(8,128)(2,1)S(1)}, bf16[8,24,2304]{2,1,0:T(8,128)(2,1)}) custom-call(s32[2]{0:T(128)S(1)} %pad_add_fusion.refs_0_, s32[1]{0:T(128)} %bitcast.refs_1_, ...), custom_call_target="tpu_custom_call" | custom-call | flops 10569646080 | bytes 20643840 | tf_op jit(solution)/shard_map/pallas_call | solution.py:511
  209.2 4.4 %all-to-all-start.1 = ((bf16[8,24,2304]{2,1,0:T(8,128)(2,1)}), bf16[8,24,2304]{2,1,0:T(8,128)(2,1)}, u32[]{:S(2)}, u32[]{:S(2)}) async-start(bf16[8,24,2304]{2,1,0:T(8,128)(2,1)} %get-tuple-element.83), calls=%async_computation.1 | async-start | bytes 1769472 | tf_op jit(solution)/shard_map/all_to_all | solution.py:733
  213.7 2.4 collective-permute-start.20
  218.8 8.6 %all-to-all-done.1 = bf16[8,24,2304]{2,1,0:T(8,128)(2,1)} async-done(((bf16[8,24,2304]{2,1,0:T(8,128)(2,1)}), bf16[8,24,2304]{2,1,0:T(8,128)(2,1)}, u32[]{:S(2)}, u32[]{:S(2)}) %all-to-all-start.1) | async-done | bytes 884768 | tf_op jit(solution)/shard_map/all_to_all | solution.py:733
  228.6 11.2 %collective-permute-done.18.refs_1_ = bf16[128,1664]{1,0:T(8,128)(2,1)} collective-permute-done((bf16[128,1664]{1,0:T(8,128)(2,1)S(1)}, bf16[128,1664]{1,0:T(8,128)(2,1)}, u32[]{:S(2)}, u32[]{:S(2)}) %collective-permute-start.18) | collective-permute-done | bytes 426016 | tf_op jit(solution)/shard_map/ppermute | solution.py:554
  239.9 12.7 %collective-permute-done.19.refs_2_ = bf16[128,1664]{1,0:T(8,128)(2,1)} collective-permute-done((bf16[128,1664]{1,0:T(8,128)(2,1)S(1)}, bf16[128,1664]{1,0:T(8,128)(2,1)}, u32[]{:S(2)}, u32[]{:S(2)}) %collective-permute-start.19) | collective-permute-done | bytes 426016 | tf_op jit(solution)/shard_map/ppermute | solution.py:554
  252.5 2.1 collective-permute-start.22
  254.7 2.3 collective-permute-start.23
  258.3 13.7 %shard_map.279 = (f32[128,1536]{1,0:T(8,128)}, bf16[128,1536]{1,0:T(8,128)(2,1)}, bf16[8,176,512]{2,1,0:T(8,128)(2,1)}, bf16[128,16]{1,0:T(8,128)(2,1)}) custom-call(bf16[128,1664]{1,0:T(8,128)(2,1)} %copy-done.4, bf16[128,1664]{1,0:T(8,128)(2,1)} %collective-permute-done.18.refs_1_, bf16[128,1664]{1,0:T(8,128)(2,1)} %collective-permute-done.19.refs_2_, ...), custom_call_target="tpu_custom_call" | custom-call | tf_op jit(solution)/shard_map/pallas_call | solution.py:165
  272.9 4.3 %all-to-all-start.2 = ((bf16[8,176,512]{2,1,0:T(8,128)(2,1)}), bf16[8,176,512]{2,1,0:T(8,128)(2,1)}, u32[]{:S(2)}, u32[]{:S(2)}) async-start(bf16[8,176,512]{2,1,0:T(8,128)(2,1)} %get-tuple-element.105), calls=%async_computation.2 | async-start | bytes 2883584 | tf_op jit(solution)/shard_map/all_to_all | solution.py:777
  278.6 18.2 %all-to-all-done.2.got_ref = bf16[8,176,512]{2,1,0:T(8,128)(2,1)} async-done(((bf16[8,176,512]{2,1,0:T(8,128)(2,1)}), bf16[8,176,512]{2,1,0:T(8,128)(2,1)}, u32[]{:S(2)}, u32[]{:S(2)}) %all-to-all-start.2) | async-done | bytes 1441824 | tf_op jit(solution)/shard_map/all_to_all | solution.py:777
  296.8 2.5 shard_map.280
  299.3 2.1 collective-permute-start.25
  301.4 2.2 collective-permute-start.26
  304.5 3.0 collective-permute-done.26
  311.1 3.6 all-to-all-start.3
  314.8 2.3 collective-permute-start.17
  317.1 2.1 collective-permute-start.16
  320.9 2.5 convolution_convert_fusion.refs_3_
  323.5 2.9 collective-permute-start.28
  326.3 2.3 collective-permute-done.17.refs_3_
  328.7 2.2 collective-permute-start.29
  334.1 6.2 %collective-permute-done.15.refs_1_ = bf16[128,1536]{1,0:T(8,128)(2,1)S(1)} collective-permute-done((bf16[128,1536]{1,0:T(8,128)(2,1)S(1)}, bf16[128,1536]{1,0:T(8,128)(2,1)S(1)}, u32[]{:S(2)}, u32[]{:S(2)}) %collective-permute-start.15) | collective-permute-done | bytes 393248 | tf_op jit(solution)/shard_map/ppermute | solution.py:554
  340.2 16.6 %collective-permute-done.16.refs_2_ = bf16[128,1536]{1,0:T(8,128)(2,1)S(1)} collective-permute-done((bf16[128,1536]{1,0:T(8,128)(2,1)S(1)}, bf16[128,1536]{1,0:T(8,128)(2,1)S(1)}, u32[]{:S(2)}, u32[]{:S(2)}) %collective-permute-start.16) | collective-permute-done | bytes 393248 | tf_op jit(solution)/shard_map/ppermute | solution.py:554
  357.6 7.5 %shard_map.281 = (bf16[128,1536]{1,0:T(8,128)(2,1)}, f32[128,1536]{1,0:T(8,128)}) custom-call(bf16[128,1536]{1,0:T(8,128)(2,1)} %copy-done.6, bf16[128,1536]{1,0:T(8,128)(2,1)} %copy-done.25, bf16[128,1536]{1,0:T(8,128)(2,1)} %copy-done.26, bf16[128,1536]{1,0:T(8,128)(2,1)} %copy-done.24, f32[128,1536]{1,0:T(8,128)} %get-tuple-element.82.refs_6_.refs_4_, ...), custom_call_target="tpu_custom_call" | custom-call | tf_op jit(solution)/shard_map/pallas_call | solution.py:165
  366.5 4.1 %shard_map.282 = (f32[4,48,1536]{2,1,0:T(8,128)}, f32[4,32,1536]{2,1,0:T(8,128)}, f32[4,16,1536]{2,1,0:T(8,128)}, f32[4,16,1536]{2,1,0:T(8,128)}, f32[4,16,1536]...) custom-call(s32[1]{0:T(128)} %bitcast.38.refs_0_, s32[4]{0:T(128)S(1)} %pad_add_fusion.2.refs_1_, ...), custom_call_target="tpu_custom_call" | custom-call | tf_op jit(solution)/shard_map/pallas_call | solution.py:154
  370.6 2.1 copy-done.2
  372.8 3.3 shard_map.283
  (177 shorter events, 63.8 us)
Async XLA Ops:
  7.2 84.1 %copy-start = (bf16[4,2,16,8960]{3,2,1,0:T(8,128)(2,1)S(1)}, bf16[4,2,16,8960]{3,2,1,0:T(8,128)(2,1)}, u32[]{:S(2)}) copy-start(bf16[4,2,16,8960]{3,2,1,0:T(8,128)(2,1)} %param.37) | copy-start | bytes 6881284
  7.2 62.2 %all-gather.10.cloned.1.call-start = ((), (), s32[]{:S(2)}) async-start(), calls=%async_computation.4 | async-start | bytes 3538944 | tf_op jit(solution)/shard_map/all_gather | solution.py:623
  11.2 100.8 %all-gather.12.cloned.1.call-start = ((), (), s32[]{:S(2)}) async-start(), calls=%async_computation.5 | async-start | bytes 5308416 | tf_op jit(solution)/shard_map/all_gather | solution.py:572
  14.9 11.4 %collective-permute-start.1 = (bf16[384,256]{1,0:T(8,128)(2,1)S(1)}, bf16[384,256]{1,0:T(8,128)(2,1)S(1)}, u32[]{:S(2)}, u32[]{:S(2)}) collective-permute-start(bf16[384,256]{1,0:T(8,128)(2,1)S(1)} %pad_maximum_fusion.5), channel_id=1, source_target_pairs={{0,1},{1,0},{2,3},{3,2},{4,5},{5,4},{6,7},{7,6},{8,9},{9,8},{10,11... | collective-permute-start | bytes 589832 | tf_op jit(solution)/shard_map/ppermute | solution.py:554
  18.0 17.2 %collective-permute-start.2 = (bf16[384,256]{1,0:T(8,128)(2,1)S(1)}, bf16[384,256]{1,0:T(8,128)(2,1)S(1)}, u32[]{:S(2)}, u32[]{:S(2)}) collective-permute-start(bf16[384,256]{1,0:T(8,128)(2,1)S(1)} %pad_maximum_fusion.5), channel_id=1, source_target_pairs={{0,2},{1,3},{2,0},{3,1},{4,6},{5,7},{6,4},{7,5},{8,10},{9,11},{10,... | collective-permute-start | bytes 589832 | tf_op jit(solution)/shard_map/ppermute | solution.py:554
  20.6 14.6 %collective-permute-start.3 = (bf16[384,256]{1,0:T(8,128)(2,1)S(1)}, bf16[384,256]{1,0:T(8,128)(2,1)S(1)}, u32[]{:S(2)}, u32[]{:S(2)}) collective-permute-start(bf16[384,256]{1,0:T(8,128)(2,1)S(1)} %pad_maximum_fusion.5), channel_id=1, source_target_pairs={{0,3},{1,2},{2,1},{3,0},{4,7},{5,6},{6,5},{7,4},{8,11},{9,10},{10,... | collective-permute-start | bytes 589832 | tf_op jit(solution)/shard_map/ppermute | solution.py:554
  41.6 8.2 %collective-permute-start.4 = (bf16[48,1536]{1,0:T(8,128)(2,1)S(1)}, bf16[48,1536]{1,0:T(8,128)(2,1)S(1)}, u32[]{:S(2)}, u32[]{:S(2)}) collective-permute-start(bf16[48,1536]{1,0:T(8,128)(2,1)S(1)} %constant_dynamic-slice_fusion.3), channel_id=1, source_target_pairs={{0,1},{1,0},{2,3},{3,2},{4,5},{5,4},{6,7},{7,6},{8,9},{9,8},{10,11... | collective-permute-start | bytes 442376 | tf_op jit(solution)/shard_map/ppermute | solution.py:554
  45.0 13.0 %collective-permute-start.5 = (bf16[48,1536]{1,0:T(8,128)(2,1)S(1)}, bf16[48,1536]{1,0:T(8,128)(2,1)S(1)}, u32[]{:S(2)}, u32[]{:S(2)}) collective-permute-start(bf16[48,1536]{1,0:T(8,128)(2,1)S(1)} %constant_dynamic-slice_fusion.3), channel_id=1, source_target_pairs={{0,2},{1,3},{2,0},{3,1},{4,6},{5,7},{6,4},{7,5},{8,10},{9,11},{10,... | collective-permute-start | bytes 442376 | tf_op jit(solution)/shard_map/ppermute | solution.py:554
  46.1 11.9 %collective-permute-start.6 = (bf16[48,1536]{1,0:T(8,128)(2,1)S(1)}, bf16[48,1536]{1,0:T(8,128)(2,1)S(1)}, u32[]{:S(2)}, u32[]{:S(2)}) collective-permute-start(bf16[48,1536]{1,0:T(8,128)(2,1)S(1)} %constant_dynamic-slice_fusion.3), channel_id=1, source_target_pairs={{0,3},{1,2},{2,1},{3,0},{4,7},{5,6},{6,5},{7,4},{8,11},{9,10},{10,... | collective-permute-start | bytes 442376 | tf_op jit(solution)/shard_map/ppermute | solution.py:554
  59.7 297.2 %all-gather.14.cloned.1.call-start = ((), (), s32[]{:S(2)}) async-start(), calls=%async_computation.6 | async-start | bytes 7077888 | tf_op jit(solution)/shard_map/all_gather | solution.py:671
  60.4 73.9 %collective-permute-start.11 = (s32[1]{0:T(128)}, s32[1]{0:T(128)}, u32[]{:S(2)}, u32[]{:S(2)}) collective-permute-start(s32[1]{0:T(128)} %param.22), channel_id=1, source_target_pairs={{0,1},{1,0},{2,3},{3,2},{4,5},{5,4},{6,7},{7,6},{8,9},{9,8},{10,11... | collective-permute-start | bytes 20 | tf_op jit(solution)/shard_map/ppermute | solution.py:554
  62.6 71.7 %collective-permute-start.12 = (s32[1]{0:T(128)}, s32[1]{0:T(128)}, u32[]{:S(2)}, u32[]{:S(2)}) collective-permute-start(s32[1]{0:T(128)} %param.22), channel_id=1, source_target_pairs={{0,2},{1,3},{2,0},{3,1},{4,6},{5,7},{6,4},{7,5},{8,10},{9,11},{10,... | collective-permute-start | bytes 20 | tf_op jit(solution)/shard_map/ppermute | solution.py:554
  74.6 42.3 %all-to-all-start = ((bf16[8,128,768]{2,1,0:T(8,128)(2,1)}), bf16[8,128,768]{2,1,0:T(8,128)(2,1)}, u32[]{:S(2)}, u32[]{:S(2)}) async-start(bf16[8,128,768]{2,1,0:T(8,128)(2,1)} %get-tuple-element.67), calls=%async_computation | async-start | bytes 3145728 | tf_op jit(solution)/shard_map/all_to_all | solution.py:668
  85.5 41.7 %collective-permute-start.7 = (bf16[128,1536]{1,0:T(8,128)(2,1)S(1)}, bf16[128,1536]{1,0:T(8,128)(2,1)S(1)}, u32[]{:S(2)}, u32[]{:S(2)}) collective-permute-start(bf16[128,1536]{1,0:T(8,128)(2,1)S(1)} %bitcast.75), channel_id=1, source_target_pairs={{0,1},{1,0},{2,3},{3,2},{4,5},{5,4},{6,7},{7,6},{8,9},{9,8},{10,11... | collective-permute-start | bytes 1179656 | tf_op jit(solution)/shard_map/ppermute | solution.py:554
  87.4 43.6 %collective-permute-start.8 = (bf16[128,1536]{1,0:T(8,128)(2,1)S(1)}, bf16[128,1536]{1,0:T(8,128)(2,1)}, u32[]{:S(2)}, u32[]{:S(2)}) collective-permute-start(bf16[128,1536]{1,0:T(8,128)(2,1)S(1)} %bitcast.76), channel_id=1, source_target_pairs={{0,2},{1,3},{2,0},{3,1},{4,6},{5,7},{6,4},{7,5},{8,10},{9,11},{10,... | collective-permute-start | bytes 1179656 | tf_op jit(solution)/shard_map/ppermute | solution.py:554
  87.7 43.3 %collective-permute-start.9 = (bf16[128,1536]{1,0:T(8,128)(2,1)S(1)}, bf16[128,1536]{1,0:T(8,128)(2,1)S(1)}, u32[]{:S(2)}, u32[]{:S(2)}) collective-permute-start(bf16[128,1536]{1,0:T(8,128)(2,1)S(1)} %bitcast.77), channel_id=1, source_target_pairs={{0,3},{1,2},{2,1},{3,0},{4,7},{5,6},{6,5},{7,4},{8,11},{9,10},{10,... | collective-permute-start | bytes 1179656 | tf_op jit(solution)/shard_map/ppermute | solution.py:554
  127.2 36.0 %copy-start.8 = (bf16[4,32,1536]{2,1,0:T(8,128)(2,1)S(1)}, bf16[4,32,1536]{2,1,0:T(8,128)(2,1)}, u32[]{:S(2)}) copy-start(bf16[4,32,1536]{2,1,0:T(8,128)(2,1)} %refs_6_.3) | copy-start | bytes 1179652
  127.2 36.0 %copy-start.9 = (bf16[4,16,1536]{2,1,0:T(8,128)(2,1)S(1)}, bf16[4,16,1536]{2,1,0:T(8,128)(2,1)}, u32[]{:S(2)}) copy-start(bf16[4,16,1536]{2,1,0:T(8,128)(2,1)} %refs_7_.3) | copy-start | bytes 589828
  127.9 5.6 %collective-permute-start = (s32[1]{0:T(128)}, s32[1]{0:T(128)}, u32[]{:S(2)}, u32[]{:S(2)}) collective-permute-start(s32[1]{0:T(128)} %param.22), channel_id=1, source_target_pairs={{0,3},{1,2},{2,1},{3,0},{4,7},{5,6},{6,5},{7,4},{8,11},{9,10},{10,... | collective-permute-start | bytes 20 | tf_op jit(solution)/shard_map/ppermute | solution.py:554
  131.0 30.9 %copy-start.14 = (bf16[128,1536]{1,0:T(8,128)(2,1)}, bf16[128,1536]{1,0:T(8,128)(2,1)S(1)}, u32[]{:S(2)}) copy-start(bf16[128,1536]{1,0:T(8,128)(2,1)S(1)} %collective-permute-done.9.refs_4_) | copy-start | bytes 1179652
  131.0 18.1 %collective-permute-start.13 = (bf16[128,1536]{1,0:T(8,128)(2,1)}, bf16[128,1536]{1,0:T(8,128)(2,1)S(1)}, u32[]{:S(2)}, u32[]{:S(2)}) collective-permute-start(bf16[128,1536]{1,0:T(8,128)(2,1)} %get-tuple-element.72.refs_3_.refs_8_), channel_id=1, source_target_pairs={{0,1},{1,0},{2,3},{3,2},{4,5},{5,4},{6,7},{7,6},{8,9},{9,8},{10,11... | collective-permute-start | bytes 1179656 | tf_op jit(solution)/shard_map/ppermute | solution.py:554
  131.1 30.0 %collective-permute-start.14 = (bf16[128,1536]{1,0:T(8,128)(2,1)}, bf16[128,1536]{1,0:T(8,128)(2,1)S(1)}, u32[]{:S(2)}, u32[]{:S(2)}) collective-permute-start(bf16[128,1536]{1,0:T(8,128)(2,1)} %get-tuple-element.72.refs_3_.refs_8_), channel_id=1, source_target_pairs={{0,2},{1,3},{2,0},{3,1},{4,6},{5,7},{6,4},{7,5},{8,10},{9,11},{10,... | collective-permute-start | bytes 1179656 | tf_op jit(solution)/shard_map/ppermute | solution.py:554
  133.5 29.7 %copy-start.17 = (bf16[128,1536]{1,0:T(8,128)(2,1)S(1)}, bf16[128,1536]{1,0:T(8,128)(2,1)}, u32[]{:S(2)}) copy-start(bf16[128,1536]{1,0:T(8,128)(2,1)} %copy-done.16) | copy-start | bytes 1179652
  135.7 50.1 %collective-permute-start.10 = (bf16[128,1536]{1,0:T(8,128)(2,1)}, bf16[128,1536]{1,0:T(8,128)(2,1)S(1)}, u32[]{:S(2)}, u32[]{:S(2)}) collective-permute-start(bf16[128,1536]{1,0:T(8,128)(2,1)} %get-tuple-element.72.refs_3_.refs_8_), channel_id=1, source_target_pairs={{0,3},{1,2},{2,1},{3,0},{4,7},{5,6},{6,5},{7,4},{8,11},{9,10},{10,... | collective-permute-start | bytes 1179656 | tf_op jit(solution)/shard_map/ppermute | solution.py:554
  209.2 18.1 %all-to-all-start.1 = ((bf16[8,24,2304]{2,1,0:T(8,128)(2,1)}), bf16[8,24,2304]{2,1,0:T(8,128)(2,1)}, u32[]{:S(2)}, u32[]{:S(2)}) async-start(bf16[8,24,2304]{2,1,0:T(8,128)(2,1)} %get-tuple-element.83), calls=%async_computation.1 | async-start | bytes 1769472 | tf_op jit(solution)/shard_map/all_to_all | solution.py:733
  213.7 15.0 %collective-permute-start.20 = (bf16[128,1664]{1,0:T(8,128)(2,1)S(1)}, bf16[128,1664]{1,0:T(8,128)(2,1)S(1)}, u32[]{:S(2)}, u32[]{:S(2)}) collective-permute-start(bf16[128,1664]{1,0:T(8,128)(2,1)S(1)} %get-tuple-element.87), channel_id=1, source_target_pairs={{0,3},{1,2},{2,1},{3,0},{4,7},{5,6},{6,5},{7,4},{8,11},{9,10},{10,... | collective-permute-start | bytes 1277960 | tf_op jit(solution)/shard_map/ppermute | solution.py:554
  216.0 23.8 %collective-permute-start.18 = (bf16[128,1664]{1,0:T(8,128)(2,1)S(1)}, bf16[128,1664]{1,0:T(8,128)(2,1)}, u32[]{:S(2)}, u32[]{:S(2)}) collective-permute-start(bf16[128,1664]{1,0:T(8,128)(2,1)S(1)} %get-tuple-element.85), channel_id=1, source_target_pairs={{0,1},{1,0},{2,3},{3,2},{4,5},{5,4},{6,7},{7,6},{8,9},{9,8},{10,11... | collective-permute-start | bytes 1277960 | tf_op jit(solution)/shard_map/ppermute | solution.py:554
  216.0 36.5 %collective-permute-start.19 = (bf16[128,1664]{1,0:T(8,128)(2,1)S(1)}, bf16[128,1664]{1,0:T(8,128)(2,1)}, u32[]{:S(2)}, u32[]{:S(2)}) collective-permute-start(bf16[128,1664]{1,0:T(8,128)(2,1)S(1)} %get-tuple-element.86), channel_id=1, source_target_pairs={{0,2},{1,3},{2,0},{3,1},{4,6},{5,7},{6,4},{7,5},{8,10},{9,11},{10,... | collective-permute-start | bytes 1277960 | tf_op jit(solution)/shard_map/ppermute | solution.py:554
  228.6 29.6 %copy-start.23 = (bf16[128,1664]{1,0:T(8,128)(2,1)}, bf16[128,1664]{1,0:T(8,128)(2,1)S(1)}, u32[]{:S(2)}) copy-start(bf16[128,1664]{1,0:T(8,128)(2,1)S(1)} %collective-permute-done.20.refs_3_) | copy-start | bytes 1277956
  252.5 19.5 %collective-permute-start.21 = (bf16[24,2304]{1,0:T(8,128)(2,1)S(1)}, bf16[24,2304]{1,0:T(8,128)(2,1)S(1)}, u32[]{:S(2)}, u32[]{:S(2)}) collective-permute-start(bf16[24,2304]{1,0:T(8,128)(2,1)S(1)} %reduce_sum.32), channel_id=1, source_target_pairs={{0,1},{1,0},{2,3},{3,2},{4,5},{5,4},{6,7},{7,6},{8,9},{9,8},{10,11... | collective-permute-start | bytes 331784 | tf_op jit(solution)/shard_map/ppermute | solution.py:554
  252.5 19.5 %collective-permute-start.22 = (bf16[24,2304]{1,0:T(8,128)(2,1)S(1)}, bf16[24,2304]{1,0:T(8,128)(2,1)S(1)}, u32[]{:S(2)}, u32[]{:S(2)}) collective-permute-start(bf16[24,2304]{1,0:T(8,128)(2,1)S(1)} %reduce_sum.32), channel_id=1, source_target_pairs={{0,2},{1,3},{2,0},{3,1},{4,6},{5,7},{6,4},{7,5},{8,10},{9,11},{10,... | collective-permute-start | bytes 331784 | tf_op jit(solution)/shard_map/ppermute | solution.py:554
  254.7 17.4 %collective-permute-start.23 = (bf16[24,2304]{1,0:T(8,128)(2,1)S(1)}, bf16[24,2304]{1,0:T(8,128)(2,1)S(1)}, u32[]{:S(2)}, u32[]{:S(2)}) collective-permute-start(bf16[24,2304]{1,0:T(8,128)(2,1)S(1)} %reduce_sum.32), channel_id=1, source_target_pairs={{0,3},{1,2},{2,1},{3,0},{4,7},{5,6},{6,5},{7,4},{8,11},{9,10},{10,... | collective-permute-start | bytes 331784 | tf_op jit(solution)/shard_map/ppermute | solution.py:554
  272.9 23.9 %all-to-all-start.2 = ((bf16[8,176,512]{2,1,0:T(8,128)(2,1)}), bf16[8,176,512]{2,1,0:T(8,128)(2,1)}, u32[]{:S(2)}, u32[]{:S(2)}) async-start(bf16[8,176,512]{2,1,0:T(8,128)(2,1)} %get-tuple-element.105), calls=%async_computation.2 | async-start | bytes 2883584 | tf_op jit(solution)/shard_map/all_to_all | solution.py:777
  277.1 37.6 %copy-start.13 = (bf16[128,1536]{1,0:T(8,128)(2,1)S(1)}, bf16[128,1536]{1,0:T(8,128)(2,1)}, u32[]{:S(2)}) copy-start(bf16[128,1536]{1,0:T(8,128)(2,1)} %copy-done.12) | copy-start | bytes 1179652
  277.1 39.9 %copy-start.11 = (bf16[128,1536]{1,0:T(8,128)(2,1)S(1)}, bf16[128,1536]{1,0:T(8,128)(2,1)}, u32[]{:S(2)}) copy-start(bf16[128,1536]{1,0:T(8,128)(2,1)} %copy-done.10) | copy-start | bytes 1179652
  277.2 87.9 %all-gather.16.cloned.1.call-start = ((), (), s32[]{:S(2)}) async-start(), calls=%async_computation.7 | async-start | bytes 1769472 | tf_op jit(solution)/shard_map/all_gather | solution.py:794
  299.3 4.4 %collective-permute-start.24 = (bf16[48,512]{1,0:T(8,128)(2,1)}, bf16[48,512]{1,0:T(8,128)(2,1)S(1)}, u32[]{:S(2)}, u32[]{:S(2)}) collective-permute-start(bf16[48,512]{1,0:T(8,128)(2,1)} %get-tuple-element.110), channel_id=1, source_target_pairs={{0,1},{1,0},{2,3},{3,2},{4,5},{5,4},{6,7},{7,6},{8,9},{9,8},{10,11... | collective-permute-start | bytes 147464 | tf_op jit(solution)/shard_map/ppermute | solution.py:554
  299.3 5.2 %collective-permute-start.25 = (bf16[48,512]{1,0:T(8,128)(2,1)}, bf16[48,512]{1,0:T(8,128)(2,1)S(1)}, u32[]{:S(2)}, u32[]{:S(2)}) collective-permute-start(bf16[48,512]{1,0:T(8,128)(2,1)} %get-tuple-element.110), channel_id=1, source_target_pairs={{0,2},{1,3},{2,0},{3,1},{4,6},{5,7},{6,4},{7,5},{8,10},{9,11},{10,... | collective-permute-start | bytes 147464 | tf_op jit(solution)/shard_map/ppermute | solution.py:554
  301.4 6.1 %collective-permute-start.26 = (bf16[48,512]{1,0:T(8,128)(2,1)}, bf16[48,512]{1,0:T(8,128)(2,1)S(1)}, u32[]{:S(2)}, u32[]{:S(2)}) collective-permute-start(bf16[48,512]{1,0:T(8,128)(2,1)} %get-tuple-element.110), channel_id=1, source_target_pairs={{0,3},{1,2},{2,1},{3,0},{4,7},{5,6},{6,5},{7,4},{8,11},{9,10},{10,... | collective-permute-start | bytes 147464 | tf_op jit(solution)/shard_map/ppermute | solution.py:554
  309.0 61.6 %all-gather.18.cloned.1.call-start = ((), (), s32[]{:S(2)}) async-start(), calls=%async_computation.8 | async-start | bytes 3981312 | tf_op jit(solution)/shard_map/all_gather | solution.py:779
  311.1 9.7 %all-to-all-start.3 = ((bf16[8,128,48]{1,2,0:T(8,128)(2,1)}), bf16[8,128,48]{1,2,0:T(8,128)(2,1)S(1)}, u32[]{:S(2)}, u32[]{:S(2)}) async-start(bf16[8,128,48]{1,2,0:T(8,128)(2,1)} %broadcast_in_dim.96), calls=%async_computation.3 | async-start | bytes 196608 | tf_op jit(solution)/shard_map/all_to_all | solution.py:793
  314.8 13.9 %collective-permute-start.17 = (bf16[128,1536]{1,0:T(8,128)(2,1)S(1)}, bf16[128,1536]{1,0:T(8,128)(2,1)S(1)}, u32[]{:S(2)}, u32[]{:S(2)}) collective-permute-start(bf16[128,1536]{1,0:T(8,128)(2,1)S(1)} %copy-done.13), channel_id=1, source_target_pairs={{0,3},{1,2},{2,1},{3,0},{4,7},{5,6},{6,5},{7,4},{8,11},{9,10},{10,... | collective-permute-start | bytes 1179656 | tf_op jit(solution)/shard_map/ppermute | solution.py:554
  317.1 23.1 %collective-permute-start.15 = (bf16[128,1536]{1,0:T(8,128)(2,1)S(1)}, bf16[128,1536]{1,0:T(8,128)(2,1)S(1)}, u32[]{:S(2)}, u32[]{:S(2)}) collective-permute-start(bf16[128,1536]{1,0:T(8,128)(2,1)S(1)} %copy-done.11), channel_id=1, source_target_pairs={{0,1},{1,0},{2,3},{3,2},{4,5},{5,4},{6,7},{7,6},{8,9},{9,8},{10,11... | collective-permute-start | bytes 1179656 | tf_op jit(solution)/shard_map/ppermute | solution.py:554
  317.1 39.7 %collective-permute-start.16 = (bf16[128,1536]{1,0:T(8,128)(2,1)S(1)}, bf16[128,1536]{1,0:T(8,128)(2,1)S(1)}, u32[]{:S(2)}, u32[]{:S(2)}) collective-permute-start(bf16[128,1536]{1,0:T(8,128)(2,1)S(1)} %get-tuple-element.80), channel_id=1, source_target_pairs={{0,2},{1,3},{2,0},{3,1},{4,6},{5,7},{6,4},{7,5},{8,10},{9,11},{10,... | collective-permute-start | bytes 1179656 | tf_op jit(solution)/shard_map/ppermute | solution.py:554
  323.4 41.6 %collective-permute-start.27 = (bf16[48,1536]{1,0:T(8,128)(2,1)S(1)}, bf16[48,1536]{1,0:T(8,128)(2,1)S(1)}, u32[]{:S(2)}, u32[]{:S(2)}) collective-permute-start(bf16[48,1536]{1,0:T(8,128)(2,1)S(1)} %convolution_convert_fusion.refs_3_), channel_id=1, source_target_pairs={{0,1},{1,0},{2,3},{3,2},{4,5},{5,4},{6,7},{7,6},{8,9},{9,8},{10,11... | collective-permute-start | bytes 442376 | tf_op jit(solution)/shard_map/ppermute | solution.py:554
  323.5 41.6 %collective-permute-start.28 = (bf16[48,1536]{1,0:T(8,128)(2,1)S(1)}, bf16[48,1536]{1,0:T(8,128)(2,1)S(1)}, u32[]{:S(2)}, u32[]{:S(2)}) collective-permute-start(bf16[48,1536]{1,0:T(8,128)(2,1)S(1)} %convolution_convert_fusion.refs_3_), channel_id=1, source_target_pairs={{0,2},{1,3},{2,0},{3,1},{4,6},{5,7},{6,4},{7,5},{8,10},{9,11},{10,... | collective-permute-start | bytes 442376 | tf_op jit(solution)/shard_map/ppermute | solution.py:554
  328.6 28.2 %copy-start.24 = (bf16[128,1536]{1,0:T(8,128)(2,1)}, bf16[128,1536]{1,0:T(8,128)(2,1)S(1)}, u32[]{:S(2)}) copy-start(bf16[128,1536]{1,0:T(8,128)(2,1)S(1)} %collective-permute-done.17.refs_3_) | copy-start | bytes 1179652
  328.7 36.4 %collective-permute-start.29 = (bf16[48,1536]{1,0:T(8,128)(2,1)S(1)}, bf16[48,1536]{1,0:T(8,128)(2,1)S(1)}, u32[]{:S(2)}, u32[]{:S(2)}) collective-permute-start(bf16[48,1536]{1,0:T(8,128)(2,1)S(1)} %convolution_convert_fusion.refs_3_), channel_id=1, source_target_pairs={{0,3},{1,2},{2,1},{3,0},{4,7},{5,6},{6,5},{7,4},{8,11},{9,10},{10,... | collective-permute-start | bytes 442376 | tf_op jit(solution)/shard_map/ppermute | solution.py:554
  (24 other events, 136.2 us)
Sparse Core Ops, SparseCore 0:
  11.3 35.0 all-gather.9
  59.8 52.1 all-gather.11
  114.5 46.0 all-gather.13
  309.2 24.2 all-gather.15
  335.8 33.9 all-gather.17
